TPU v7x, 128 devices: a whole 4x4x4 slice. The times are simulated.
128 devices in a mesh: tm: 8 (over z_hi, x), gx: 16 (over z_lo, y, core).
Axes of the slice: x: 4, y: 4, z: 4 (z_hi: 2, z_lo: 2; z = z_hi * 2 + z_lo), core: 2. Of those that a mesh axis runs over, the one named last changes fastest.
Arguments:
- state: float32 [16, 64, 256, 128], P('tm', 'gx'), may hold values from -3 to 3
- start_field: float32 [64, 256, 128], P('gx'), may hold values from -3 to 3
- diffusivity: float32 [64, 256, 128], P('gx'), may hold values from 0.3 to 3
- time_weights: float32 [16], P('tm'), may hold values from 0.4 to 1
- shift_real: float32 [16], replicated, may hold values from 0.5 to 2, as said below
- shift_imag: float32 [16], replicated, may hold values from -1 to 1, as said below
Outputs:
- new_state: float32 [16, 64, 256, 128], P('tm', 'gx')
Inputs may be any that keep to these rules, and one draw needn't show every extreme that they name: `shift_real`: shift_real_k = shift_real_(16 - k) for k = 1 .. 15. `shift_imag`: shift_imag_0 = shift_imag_(8) = 0 and shift_imag_k = - shift_imag_(16 - k), so the eigenvalues come in conjugate pairs.
All inputs are finite; a program needn't handle non-finite values.
Results may differ from a plain program's by a relative error of at most 0.0003.
Values sent between devices are 32-bit elements; how exact they have to be, the bound alone decides.
A program may use at most 64 MiB of HBM per device.

v0:
```python
import math

import jax
import jax.numpy as jnp
from jax import lax
from jax.sharding import PartitionSpec as P

SWEEPS = 12


cheb_centre = 1.0
cheb_half = 0.7


def swapped(value, axis, stride):
    mask = 2**stride
    pairs = [(source, source ^ mask) for source in range(lax.axis_size(axis))]
    return lax.ppermute(value, axis, pairs)


def padded_2(block, sides, width):
    for axis, dim in sides:
        count = lax.axis_size(axis)
        forward = [(i, i + 1) for i in range(count - 1)]
        backward = [(target, source) for source, target in forward]
        low = lax.ppermute(
            lax.slice_in_dim(block, block.shape[dim] - width, None, axis=dim), axis, forward
        )
        high = lax.ppermute(lax.slice_in_dim(block, 0, width, axis=dim), axis, backward)
        block = jnp.concatenate([low, block, high], axis=dim)
    return block


def shifted(value, axis, steps):
    count = lax.axis_size(axis)
    initial, last = (max(0, -steps), min(count, count - steps))
    return lax.ppermute(value, axis, [(source, source + steps) for source in range(initial, last)])


def along(core, axis, lower):
    length = core.shape[axis]
    zeros = jnp.zeros_like(lax.slice_in_dim(core, 0, 1, axis=axis))
    if lower:
        return jnp.concatenate([zeros, lax.slice_in_dim(core, 0, length - 1, axis=axis)], axis)
    return jnp.concatenate([lax.slice_in_dim(core, 1, length, axis=axis), zeros], axis)


def six_near(padded):
    core = padded[..., 1:-1, :, :]
    rank = core.ndim
    return (
        core,
        (
            padded[..., :-2, :, :],
            padded[..., 2:, :, :],
            along(core, rank - 2, True),
            along(core, rank - 2, False),
            along(core, rank - 1, True),
            along(core, rank - 1, False),
        ),
    )


def operate(padded, faces, diag_sum):
    core, near = six_near(padded)
    total = faces[0] * near[0]
    for which in range(1, 6):
        total = total + faces[which] * near[which]
    return diag_sum * core - total


def rotate(field, exponent, total_steps, sign):
    angle = exponent.astype(jnp.float32) * (sign * 2.0 * math.pi / total_steps)
    cosine = jnp.cos(angle).reshape((-1, 1, 1, 1))
    sine = jnp.sin(angle).reshape((-1, 1, 1, 1))
    real_part = field[..., 0, :, :, :]
    imag_part = field[..., 1, :, :, :]
    return jnp.stack(
        [real_part * cosine - imag_part * sine, real_part * sine + imag_part * cosine], -4
    )


def reversed_bits(position, places):
    result = jnp.zeros_like(position)
    for place in range(places):
        result = result | (position >> place & 1) << places - 1 - place
    return result


def forward_butterfly(field, total_steps):
    local_steps = field.shape[0]
    device = lax.axis_index("tm")
    position = device * local_steps + lax.iota(jnp.int32, local_steps)
    levels = lax.axis_size("tm").bit_length() - 1
    for level in range(levels - 1, -1, -1):
        span = local_steps * (1 << level)
        partner = swapped(field, "tm", level)
        upper = device >> level & 1
        sign = (1 - 2 * upper).astype(jnp.float32)
        exponent = position % span * (total_steps // (2 * span)) * upper
        field = rotate(partner + sign * field, exponent, total_steps, -1.0)
    span = local_steps // 2
    while span >= 1:
        grouped = field.reshape((local_steps // (2 * span), 2, span) + field.shape[1:])
        first = grouped[:, 0]
        second = grouped[:, 1]
        exponent = lax.iota(jnp.int32, span) * (total_steps // (2 * span))
        field = jnp.stack(
            [first + second, rotate(first - second, exponent, total_steps, -1.0)], 1
        ).reshape(field.shape)
        span = span // 2
    return field


def inverse_butterfly(field, total_steps):
    local_steps = field.shape[0]
    span = 1
    while span < local_steps:
        grouped = field.reshape((local_steps // (2 * span), 2, span) + field.shape[1:])
        first = grouped[:, 0]
        second = grouped[:, 1]
        exponent = lax.iota(jnp.int32, span) * (total_steps // (2 * span))
        turned = rotate(second, exponent, total_steps, 1.0)
        field = jnp.stack([first + turned, first - turned], 1).reshape(field.shape)
        span = span * 2
    device = lax.axis_index("tm")
    position = device * local_steps + lax.iota(jnp.int32, local_steps)
    levels = lax.axis_size("tm").bit_length() - 1
    for level in range(levels):
        span = local_steps * (1 << level)
        partner = swapped(field, "tm", level)
        upper = device >> level & 1
        sign = (1 - 2 * upper).astype(jnp.float32)
        flag = upper == 1
        exponent = position % span * (total_steps // (2 * span))
        turned = rotate(jnp.where(flag, field, partner), exponent, total_steps, 1.0)
        field = jnp.where(flag, partner, field) + sign * turned
    return field


def shards(state, start_field, diffusivity, time_weights, shift_real, shift_imag):
    local_steps = state.shape[0]
    total_steps = local_steps * lax.axis_size("tm")
    device = lax.axis_index("tm")
    stacked = jnp.concatenate([diffusivity[None], state], 0)
    padded = padded_2(stacked, (("gx", 1),), 1)
    kappa, near = six_near(padded[0])
    faces = [0.5 * (kappa + other) for other in near]
    diag_sum = faces[0]
    for which in range(1, 6):
        diag_sum = diag_sum + faces[which]
    carried = shifted(state[local_steps - 1], "tm", 1)
    first_prior = jnp.where(device == 0, start_field, carried)
    prior = jnp.concatenate([first_prior[None], state[: local_steps - 1]], 0)
    applied = operate(padded[1:], faces, diag_sum)
    residual = prior - state - (applied + state * state * state - state)
    weighted = time_weights[:, None, None, None] * residual
    field = jnp.stack([weighted, jnp.zeros_like(weighted)], 1)
    local_index = device * local_steps + lax.iota(jnp.int32, local_steps)
    spectral = forward_butterfly(field, total_steps)
    mode = reversed_bits(local_index, total_steps.bit_length() - 1)
    chooser = (mode[:, None] == lax.iota(jnp.int32, total_steps)[None, :]).astype(jnp.float32)
    mode_real = jnp.dot(
        chooser, shift_real, precision=lax.Precision.HIGHEST, preferred_element_type=jnp.float32
    ).reshape((-1, 1, 1, 1))
    mode_imag = jnp.dot(
        chooser, shift_imag, precision=lax.Precision.HIGHEST, preferred_element_type=jnp.float32
    ).reshape((-1, 1, 1, 1))
    denom_real = mode_real + diag_sum
    magnitude = denom_real * denom_real + mode_imag * mode_imag
    inverse_real = denom_real / magnitude
    inverse_imag = -mode_imag / magnitude
    source_real = spectral[:, 0]
    source_imag = spectral[:, 1]
    solution = jnp.stack(
        [
            source_real * inverse_real - source_imag * inverse_imag,
            source_real * inverse_imag + source_imag * inverse_real,
        ],
        1,
    )

    def sweep(turn, current):
        omega = 1.0 / (
            cheb_centre
            + cheb_half * jnp.cos(math.pi * (2.0 * turn.astype(jnp.float32) + 1.0) / (2.0 * SWEEPS))
        )
        extended = padded_2(current, (("gx", 2),), 1)
        image = operate(extended, faces, diag_sum)
        answer_real = current[:, 0]
        answer_imag = current[:, 1]
        misfit_real = source_real - (
            mode_real * answer_real - mode_imag * answer_imag + image[:, 0]
        )
        misfit_imag = source_imag - (
            mode_real * answer_imag + mode_imag * answer_real + image[:, 1]
        )
        return jnp.stack(
            [
                answer_real + omega * (misfit_real * inverse_real - misfit_imag * inverse_imag),
                answer_imag + omega * (misfit_real * inverse_imag + misfit_imag * inverse_real),
            ],
            1,
        )

    solution = lax.fori_loop(0, SWEEPS, sweep, solution)
    back = inverse_butterfly(solution, total_steps)
    delta = back[:, 0] / (total_steps * time_weights[:, None, None, None])
    return state + delta


def solution(mesh):
    in_specs = (
        P("tm", "gx", None, None),
        P("gx", None, None),
        P("gx", None, None),
        P("tm"),
        P(),
        P(),
    )
    out_specs = P("tm", "gx", None, None)
    return jax.shard_map(shards, mesh=mesh, in_specs=in_specs, out_specs=out_specs, check_vma=False)
```

profile of v0, /device:TPU:91, one launch (start us, length us, event | category | flops | bytes accessed | tf_op | source)
XLA Modules:
  0.0 598.0 jit_solution(1606851007833691997)
XLA Ops:
  1.3 3.5 collective-permute-start.3
  9.8 6.3 %collective-permute-done.4 = f32[3,1,256,128]{3,2,1,0:T(8,128)S(1)} collective-permute-done((f32[3,1,256,128]{3,2,1,0:T(8,128)S(1)}, f32[3,1,256,128]{3,2,1,0:T(8,128)S(1)}, u32[]{:S(2)}, u32[]{:S(2)}) %collective-permute-start.4) | collective-permute-done | bytes 393248 | tf_op jit(solution)/shard_map/ppermute | solution.py:29
  16.3 3.3 collective-permute-start.2
  21.2 8.1 %collective-permute-done.2 = f32[4,256,128]{2,1,0:T(8,128)S(1)} collective-permute-done((f32[4,256,128]{2,1,0:T(8,128)S(1)}, f32[4,256,128]{2,1,0:T(8,128)S(1)}, u32[]{:S(2)}, u32[]{:S(2)}) %collective-permute-start.2) | collective-permute-done | bytes 524320 | tf_op jit(solution)/shard_map/ppermute | solution.py:37
  32.6 47.4 %collective-permute-done.5 = f32[2,2,4,256,128]{4,3,2,0,1:T(8,128)S(1)} collective-permute-done((f32[2,2,4,256,128]{4,3,2,0,1:T(8,128)}, f32[2,2,4,256,128]{4,3,2,0,1:T(8,128)S(1)}, u32[]{:S(2)}, u32[]{:S(2)}) %collective-permute-start.5) | collective-permute-done | bytes 2097184 | tf_op jit(solution)/shard_map/ppermute | solution.py:18
  85.3 46.7 %collective-permute-done.6 = f32[2,2,4,256,128]{4,3,2,0,1:T(8,128)} collective-permute-done((f32[2,2,4,256,128]{4,3,2,0,1:T(8,128)}, f32[2,2,4,256,128]{4,3,2,0,1:T(8,128)}, u32[]{:S(2)}, u32[]{:S(2)}) %collective-permute-start.6) | collective-permute-done | bytes 2097184 | tf_op jit(solution)/shard_map/ppermute | solution.py:18
  135.9 3.9 collective-permute-start.7
  140.2 45.7 %collective-permute-done.7 = f32[2,2,4,256,128]{4,3,2,0,1:T(8,128)} collective-permute-done((f32[2,2,4,256,128]{4,3,2,0,1:T(8,128)}, f32[2,2,4,256,128]{4,3,2,0,1:T(8,128)}, u32[]{:S(2)}, u32[]{:S(2)}) %collective-permute-start.7) | collective-permute-done | bytes 2097184 | tf_op jit(solution)/shard_map/ppermute | solution.py:18
  191.0 249.8 %while.17 = (s32[]{:T(128)}, f32[2,2,4,256,128]{4,3,2,1,0:T(8,128)S(1)}, f32[2,4,256,128]{3,2,1,0:T(8,128)}, f32[2,1,1,1]{0,3,2,1:T(1,128)S(1)}, f32[2,1,1,1]{0,...) while((s32[]{:T(128)}, ...), condition=%wide.region_1.2_spmd.clone.clone, body=%wide.region_0.1_spmd.clone.clone.sunk | while | flops 16252937 | bytes 94618288 | solution.py:206
  194.7 5.1 collective-permute-start.1
  199.8 2.8 fusion.89
  206.3 3.4 fusion.91
  214.2 6.5 %collective-permute-start.1 = (f32[2,2,1,256,128]{4,3,2,1,0:T(8,128)}, f32[2,2,1,256,128]{4,3,2,1,0:T(8,128)}, u32[]{:S(2)}, u32[]{:S(2)}) collective-permute-start(f32[2,2,1,256,128]{4,3,2,1,0:T(8,128)} %get-tuple-element.654), channel_id=1, source_target_pairs={{0,1},{1,2},{2,3},{3,4},{4,5},{5,6},{6,7},{7,8},{8,9},{9,10},{10,1... | collective-permute-start | bytes 1572872 | tf_op jit(solution)/shard_map/while/body/eval_jaxpr/ppermute | solution.py:26
  220.7 2.8 fusion.89
  227.2 3.4 fusion.91
  235.1 6.5 %collective-permute-start.1 = (f32[2,2,1,256,128]{4,3,2,1,0:T(8,128)}, f32[2,2,1,256,128]{4,3,2,1,0:T(8,128)}, u32[]{:S(2)}, u32[]{:S(2)}) collective-permute-start(f32[2,2,1,256,128]{4,3,2,1,0:T(8,128)} %get-tuple-element.654), channel_id=1, source_target_pairs={{0,1},{1,2},{2,3},{3,4},{4,5},{5,6},{6,7},{7,8},{8,9},{9,10},{10,1... | collective-permute-start | bytes 1572872 | tf_op jit(solution)/shard_map/while/body/eval_jaxpr/ppermute | solution.py:26
  241.6 2.8 fusion.89
  248.1 3.4 fusion.91
  255.9 6.5 %collective-permute-start.1 = (f32[2,2,1,256,128]{4,3,2,1,0:T(8,128)}, f32[2,2,1,256,128]{4,3,2,1,0:T(8,128)}, u32[]{:S(2)}, u32[]{:S(2)}) collective-permute-start(f32[2,2,1,256,128]{4,3,2,1,0:T(8,128)} %get-tuple-element.654), channel_id=1, source_target_pairs={{0,1},{1,2},{2,3},{3,4},{4,5},{5,6},{6,7},{7,8},{8,9},{9,10},{10,1... | collective-permute-start | bytes 1572872 | tf_op jit(solution)/shard_map/while/body/eval_jaxpr/ppermute | solution.py:26
  262.4 2.8 fusion.89
  268.9 3.4 fusion.91
  276.8 6.5 %collective-permute-start.1 = (f32[2,2,1,256,128]{4,3,2,1,0:T(8,128)}, f32[2,2,1,256,128]{4,3,2,1,0:T(8,128)}, u32[]{:S(2)}, u32[]{:S(2)}) collective-permute-start(f32[2,2,1,256,128]{4,3,2,1,0:T(8,128)} %get-tuple-element.654), channel_id=1, source_target_pairs={{0,1},{1,2},{2,3},{3,4},{4,5},{5,6},{6,7},{7,8},{8,9},{9,10},{10,1... | collective-permute-start | bytes 1572872 | tf_op jit(solution)/shard_map/while/body/eval_jaxpr/ppermute | solution.py:26
  283.3 2.8 fusion.89
  289.8 3.4 fusion.91
  297.7 6.5 %collective-permute-start.1 = (f32[2,2,1,256,128]{4,3,2,1,0:T(8,128)}, f32[2,2,1,256,128]{4,3,2,1,0:T(8,128)}, u32[]{:S(2)}, u32[]{:S(2)}) collective-permute-start(f32[2,2,1,256,128]{4,3,2,1,0:T(8,128)} %get-tuple-element.654), channel_id=1, source_target_pairs={{0,1},{1,2},{2,3},{3,4},{4,5},{5,6},{6,7},{7,8},{8,9},{9,10},{10,1... | collective-permute-start | bytes 1572872 | tf_op jit(solution)/shard_map/while/body/eval_jaxpr/ppermute | solution.py:26
  304.2 2.8 fusion.89
  310.7 3.4 fusion.91
  318.6 6.5 %collective-permute-start.1 = (f32[2,2,1,256,128]{4,3,2,1,0:T(8,128)}, f32[2,2,1,256,128]{4,3,2,1,0:T(8,128)}, u32[]{:S(2)}, u32[]{:S(2)}) collective-permute-start(f32[2,2,1,256,128]{4,3,2,1,0:T(8,128)} %get-tuple-element.654), channel_id=1, source_target_pairs={{0,1},{1,2},{2,3},{3,4},{4,5},{5,6},{6,7},{7,8},{8,9},{9,10},{10,1... | collective-permute-start | bytes 1572872 | tf_op jit(solution)/shard_map/while/body/eval_jaxpr/ppermute | solution.py:26
  325.1 2.8 fusion.89
  331.6 3.4 fusion.91
  339.4 6.5 %collective-permute-start.1 = (f32[2,2,1,256,128]{4,3,2,1,0:T(8,128)}, f32[2,2,1,256,128]{4,3,2,1,0:T(8,128)}, u32[]{:S(2)}, u32[]{:S(2)}) collective-permute-start(f32[2,2,1,256,128]{4,3,2,1,0:T(8,128)} %get-tuple-element.654), channel_id=1, source_target_pairs={{0,1},{1,2},{2,3},{3,4},{4,5},{5,6},{6,7},{7,8},{8,9},{9,10},{10,1... | collective-permute-start | bytes 1572872 | tf_op jit(solution)/shard_map/while/body/eval_jaxpr/ppermute | solution.py:26
  346.0 2.8 fusion.89
  352.4 3.4 fusion.91
  360.3 6.5 %collective-permute-start.1 = (f32[2,2,1,256,128]{4,3,2,1,0:T(8,128)}, f32[2,2,1,256,128]{4,3,2,1,0:T(8,128)}, u32[]{:S(2)}, u32[]{:S(2)}) collective-permute-start(f32[2,2,1,256,128]{4,3,2,1,0:T(8,128)} %get-tuple-element.654), channel_id=1, source_target_pairs={{0,1},{1,2},{2,3},{3,4},{4,5},{5,6},{6,7},{7,8},{8,9},{9,10},{10,1... | collective-permute-start | bytes 1572872 | tf_op jit(solution)/shard_map/while/body/eval_jaxpr/ppermute | solution.py:26
  366.8 2.8 fusion.89
  373.3 3.4 fusion.91
  381.2 6.5 %collective-permute-start.1 = (f32[2,2,1,256,128]{4,3,2,1,0:T(8,128)}, f32[2,2,1,256,128]{4,3,2,1,0:T(8,128)}, u32[]{:S(2)}, u32[]{:S(2)}) collective-permute-start(f32[2,2,1,256,128]{4,3,2,1,0:T(8,128)} %get-tuple-element.654), channel_id=1, source_target_pairs={{0,1},{1,2},{2,3},{3,4},{4,5},{5,6},{6,7},{7,8},{8,9},{9,10},{10,1... | collective-permute-start | bytes 1572872 | tf_op jit(solution)/shard_map/while/body/eval_jaxpr/ppermute | solution.py:26
  394.2 3.4 fusion.91
  402.1 6.5 %collective-permute-start.1 = (f32[2,2,1,256,128]{4,3,2,1,0:T(8,128)}, f32[2,2,1,256,128]{4,3,2,1,0:T(8,128)}, u32[]{:S(2)}, u32[]{:S(2)}) collective-permute-start(f32[2,2,1,256,128]{4,3,2,1,0:T(8,128)} %get-tuple-element.654), channel_id=1, source_target_pairs={{0,1},{1,2},{2,3},{3,4},{4,5},{5,6},{6,7},{7,8},{8,9},{9,10},{10,1... | collective-permute-start | bytes 1572872 | tf_op jit(solution)/shard_map/while/body/eval_jaxpr/ppermute | solution.py:26
  415.1 3.4 fusion.91
  422.9 6.5 %collective-permute-start.1 = (f32[2,2,1,256,128]{4,3,2,1,0:T(8,128)}, f32[2,2,1,256,128]{4,3,2,1,0:T(8,128)}, u32[]{:S(2)}, u32[]{:S(2)}) collective-permute-start(f32[2,2,1,256,128]{4,3,2,1,0:T(8,128)} %get-tuple-element.654), channel_id=1, source_target_pairs={{0,1},{1,2},{2,3},{3,4},{4,5},{5,6},{6,7},{7,8},{8,9},{9,10},{10,1... | collective-permute-start | bytes 1572872 | tf_op jit(solution)/shard_map/while/body/eval_jaxpr/ppermute | solution.py:26
  435.9 3.4 fusion.91
  444.1 42.2 %collective-permute-done.8 = f32[2,2,4,256,128]{4,3,2,0,1:T(8,128)} collective-permute-done((f32[2,2,4,256,128]{4,3,2,0,1:T(8,128)}, f32[2,2,4,256,128]{4,3,2,0,1:T(8,128)}, u32[]{:S(2)}, u32[]{:S(2)}) %collective-permute-start.8) | collective-permute-done | bytes 2097184 | tf_op jit(solution)/shard_map/ppermute | solution.py:18
  487.0 3.9 fusion.28
  491.0 45.9 %collective-permute-done.9 = f32[2,2,4,256,128]{4,3,2,0,1:T(8,128)} collective-permute-done((f32[2,2,4,256,128]{4,3,2,0,1:T(8,128)}, f32[2,2,4,256,128]{4,3,2,0,1:T(8,128)}, u32[]{:S(2)}, u32[]{:S(2)}) %collective-permute-start.9) | collective-permute-done | bytes 2097184 | tf_op jit(solution)/shard_map/ppermute | solution.py:18
  536.9 3.4 broadcast_select_fusion.1
  541.5 3.8 fusion.29
  545.4 46.9 %collective-permute-done.10 = f32[2,2,4,256,128]{4,3,2,0,1:T(8,128)S(1)} collective-permute-done((f32[2,2,4,256,128]{4,3,2,0,1:T(8,128)}, f32[2,2,4,256,128]{4,3,2,0,1:T(8,128)S(1)}, u32[]{:S(2)}, u32[]{:S(2)}) %collective-permute-start.10) | collective-permute-done | bytes 2097184 | tf_op jit(solution)/shard_map/ppermute | solution.py:18
  (405 shorter events, 141.3 us)
Async XLA Ops:
  0.0 140.1 %copy-start = (f32[16]{0:T(128)S(1)}, f32[16]{0:T(128)}, u32[]{:S(2)}) copy-start(f32[16]{0:T(128)} %param.13) | copy-start | bytes 196
  0.0 6.8 %copy-start.4 = (f32[2,4,256,128]{3,2,1,0:T(8,128)S(1)}, f32[2,4,256,128]{3,2,1,0:T(8,128)}, u32[]{:S(2)}) copy-start(f32[2,4,256,128]{3,2,1,0:T(8,128)} %param.8) | copy-start | bytes 3145732
  1.3 8.6 %collective-permute-start.3 = (f32[3,1,256,128]{3,2,1,0:T(8,128)S(1)}, f32[3,1,256,128]{3,2,1,0:T(8,128)S(1)}, u32[]{:S(2)}, u32[]{:S(2)}) collective-permute-start(f32[3,1,256,128]{3,2,1,0:T(8,128)S(1)} %get-tuple-element.516), channel_id=1, source_target_pairs={{0,1},{1,2},{2,3},{3,4},{4,5},{5,6},{6,7},{7,8},{8,9},{9,10},{10,1... | collective-permute-start | bytes 1179656 | tf_op jit(solution)/shard_map/ppermute | solution.py:26
  4.7 3.6 copy-start.6
  4.7 11.3 %collective-permute-start.4 = (f32[3,1,256,128]{3,2,1,0:T(8,128)S(1)}, f32[3,1,256,128]{3,2,1,0:T(8,128)S(1)}, u32[]{:S(2)}, u32[]{:S(2)}) collective-permute-start(f32[3,1,256,128]{3,2,1,0:T(8,128)S(1)} %get-tuple-element.517), channel_id=1, source_target_pairs={{1,0},{2,1},{3,2},{4,3},{5,4},{6,5},{7,6},{8,7},{9,8},{10,9},{11,1... | collective-permute-start | bytes 1179656 | tf_op jit(solution)/shard_map/ppermute | solution.py:29
  16.3 13.0 %collective-permute-start.2 = (f32[4,256,128]{2,1,0:T(8,128)S(1)}, f32[4,256,128]{2,1,0:T(8,128)S(1)}, u32[]{:S(2)}, u32[]{:S(2)}) collective-permute-start(f32[4,256,128]{2,1,0:T(8,128)S(1)} %get-tuple-element.523), channel_id=1, source_target_pairs={{0,16},{16,32},{32,48},{48,64},{64,80},{80,96},{96,112},{1,17},{17... | collective-permute-start | bytes 1572872 | tf_op jit(solution)/shard_map/ppermute | solution.py:37
  19.6 9.6 %copy-start.24 = (f32[4,256,128]{2,1,0:T(8,128)S(1)}, f32[4,256,128]{2,1,0:T(8,128)}, u32[]{:S(2)}) copy-start(f32[4,256,128]{2,1,0:T(8,128)} %param.9) | copy-start | bytes 1572868
  19.7 9.7 %copy-start.21 = (f32[2,4,255,128]{3,2,1,0:T(8,128)S(1)}, f32[2,4,255,128]{3,2,1,0:T(8,128)}, u32[]{:S(2)}) copy-start(f32[2,4,255,128]{3,2,1,0:T(8,128)} %get-tuple-element.525) | copy-start | bytes 3133444
  19.7 9.7 %copy-start.25 = (f32[2]{0:T(128)S(1)}, f32[2]{0:T(128)}, u32[]{:S(2)}) copy-start(f32[2]{0:T(128)} %param.11) | copy-start | bytes 28
  21.2 9.7 %copy-start.9 = (f32[4,256,128]{2,1,0:T(8,128)}, f32[4,256,128]{2,1,0:T(8,128)S(1)}, u32[]{:S(2)}) copy-start(f32[4,256,128]{2,1,0:T(8,128)S(1)} %get-tuple-element.671) | copy-start | bytes 1572868
  21.2 9.7 %copy-start.11 = (f32[4,256,128]{2,1,0:T(8,128)}, f32[4,256,128]{2,1,0:T(8,128)S(1)}, u32[]{:S(2)}) copy-start(f32[4,256,128]{2,1,0:T(8,128)S(1)} %get-tuple-element.672) | copy-start | bytes 1572868
  21.2 9.7 %copy-start.13 = (f32[4,256,128]{2,1,0:T(8,128)}, f32[4,256,128]{2,1,0:T(8,128)S(1)}, u32[]{:S(2)}) copy-start(f32[4,256,128]{2,1,0:T(8,128)S(1)} %get-tuple-element.673) | copy-start | bytes 1572868
  21.2 8.2 %copy-start.20 = (f32[2,4,255,128]{3,2,1,0:T(8,128)S(1)}, f32[2,4,255,128]{3,2,1,0:T(8,128)}, u32[]{:S(2)}) copy-start(f32[2,4,255,128]{3,2,1,0:T(8,128)} %get-tuple-element.524) | copy-start | bytes 3133444
  32.6 47.5 %collective-permute-start.5 = (f32[2,2,4,256,128]{4,3,2,0,1:T(8,128)}, f32[2,2,4,256,128]{4,3,2,0,1:T(8,128)S(1)}, u32[]{:S(2)}, u32[]{:S(2)}) collective-permute-start(f32[2,2,4,256,128]{4,3,2,0,1:T(8,128)} %stack.84), channel_id=1, source_target_pairs={{0,64},{16,80},{32,96},{48,112},{64,0},{80,16},{96,32},{112,48},{1... | collective-permute-start | bytes 6291464 | tf_op jit(solution)/shard_map/ppermute | solution.py:18
  83.4 48.6 %collective-permute-start.6 = (f32[2,2,4,256,128]{4,3,2,0,1:T(8,128)}, f32[2,2,4,256,128]{4,3,2,0,1:T(8,128)}, u32[]{:S(2)}, u32[]{:S(2)}) collective-permute-start(f32[2,2,4,256,128]{4,3,2,0,1:T(8,128)} %pad_maximum_fusion.3), channel_id=1, source_target_pairs={{0,32},{16,48},{32,0},{48,16},{64,96},{80,112},{96,64},{112,80},{1... | collective-permute-start | bytes 6291464 | tf_op jit(solution)/shard_map/ppermute | solution.py:18
  134.4 5.4 copy-start.26
  135.9 50.1 %collective-permute-start.7 = (f32[2,2,4,256,128]{4,3,2,0,1:T(8,128)}, f32[2,2,4,256,128]{4,3,2,0,1:T(8,128)}, u32[]{:S(2)}, u32[]{:S(2)}) collective-permute-start(f32[2,2,4,256,128]{4,3,2,0,1:T(8,128)} %pad_maximum_fusion.4), channel_id=1, source_target_pairs={{0,16},{16,0},{32,48},{48,32},{64,80},{80,64},{96,112},{112,96},{1... | collective-permute-start | bytes 6291464 | tf_op jit(solution)/shard_map/ppermute | solution.py:18
  192.1 12.9 %collective-permute-start = (f32[2,2,1,256,128]{4,3,2,1,0:T(8,128)}, f32[2,2,1,256,128]{4,3,2,1,0:T(8,128)}, u32[]{:S(2)}, u32[]{:S(2)}) collective-permute-start(f32[2,2,1,256,128]{4,3,2,1,0:T(8,128)} %get-tuple-element.653), channel_id=1, source_target_pairs={{1,0},{2,1},{3,2},{4,3},{5,4},{6,5},{7,6},{8,7},{9,8},{10,9},{11,1... | collective-permute-start | bytes 1572872 | tf_op jit(solution)/shard_map/while/body/eval_jaxpr/ppermute | solution.py:29
  194.7 11.5 %collective-permute-start.1 = (f32[2,2,1,256,128]{4,3,2,1,0:T(8,128)}, f32[2,2,1,256,128]{4,3,2,1,0:T(8,128)}, u32[]{:S(2)}, u32[]{:S(2)}) collective-permute-start(f32[2,2,1,256,128]{4,3,2,1,0:T(8,128)} %get-tuple-element.654), channel_id=1, source_target_pairs={{0,1},{1,2},{2,3},{3,4},{4,5},{5,6},{6,7},{7,8},{8,9},{9,10},{10,1... | collective-permute-start | bytes 1572872 | tf_op jit(solution)/shard_map/while/body/eval_jaxpr/ppermute | solution.py:26
  202.7 3.5 copy-start.2
  212.3 13.7 %collective-permute-start = (f32[2,2,1,256,128]{4,3,2,1,0:T(8,128)}, f32[2,2,1,256,128]{4,3,2,1,0:T(8,128)}, u32[]{:S(2)}, u32[]{:S(2)}) collective-permute-start(f32[2,2,1,256,128]{4,3,2,1,0:T(8,128)} %get-tuple-element.653), channel_id=1, source_target_pairs={{1,0},{2,1},{3,2},{4,3},{5,4},{6,5},{7,6},{8,7},{9,8},{10,9},{11,1... | collective-permute-start | bytes 1572872 | tf_op jit(solution)/shard_map/while/body/eval_jaxpr/ppermute | solution.py:29
  214.2 12.9 %collective-permute-start.1 = (f32[2,2,1,256,128]{4,3,2,1,0:T(8,128)}, f32[2,2,1,256,128]{4,3,2,1,0:T(8,128)}, u32[]{:S(2)}, u32[]{:S(2)}) collective-permute-start(f32[2,2,1,256,128]{4,3,2,1,0:T(8,128)} %get-tuple-element.654), channel_id=1, source_target_pairs={{0,1},{1,2},{2,3},{3,4},{4,5},{5,6},{6,7},{7,8},{8,9},{9,10},{10,1... | collective-permute-start | bytes 1572872 | tf_op jit(solution)/shard_map/while/body/eval_jaxpr/ppermute | solution.py:26
  233.1 13.7 %collective-permute-start = (f32[2,2,1,256,128]{4,3,2,1,0:T(8,128)}, f32[2,2,1,256,128]{4,3,2,1,0:T(8,128)}, u32[]{:S(2)}, u32[]{:S(2)}) collective-permute-start(f32[2,2,1,256,128]{4,3,2,1,0:T(8,128)} %get-tuple-element.653), channel_id=1, source_target_pairs={{1,0},{2,1},{3,2},{4,3},{5,4},{6,5},{7,6},{8,7},{9,8},{10,9},{11,1... | collective-permute-start | bytes 1572872 | tf_op jit(solution)/shard_map/while/body/eval_jaxpr/ppermute | solution.py:29
  235.1 12.9 %collective-permute-start.1 = (f32[2,2,1,256,128]{4,3,2,1,0:T(8,128)}, f32[2,2,1,256,128]{4,3,2,1,0:T(8,128)}, u32[]{:S(2)}, u32[]{:S(2)}) collective-permute-start(f32[2,2,1,256,128]{4,3,2,1,0:T(8,128)} %get-tuple-element.654), channel_id=1, source_target_pairs={{0,1},{1,2},{2,3},{3,4},{4,5},{5,6},{6,7},{7,8},{8,9},{9,10},{10,1... | collective-permute-start | bytes 1572872 | tf_op jit(solution)/shard_map/while/body/eval_jaxpr/ppermute | solution.py:26
  254.0 13.7 %collective-permute-start = (f32[2,2,1,256,128]{4,3,2,1,0:T(8,128)}, f32[2,2,1,256,128]{4,3,2,1,0:T(8,128)}, u32[]{:S(2)}, u32[]{:S(2)}) collective-permute-start(f32[2,2,1,256,128]{4,3,2,1,0:T(8,128)} %get-tuple-element.653), channel_id=1, source_target_pairs={{1,0},{2,1},{3,2},{4,3},{5,4},{6,5},{7,6},{8,7},{9,8},{10,9},{11,1... | collective-permute-start | bytes 1572872 | tf_op jit(solution)/shard_map/while/body/eval_jaxpr/ppermute | solution.py:29
  255.9 12.9 %collective-permute-start.1 = (f32[2,2,1,256,128]{4,3,2,1,0:T(8,128)}, f32[2,2,1,256,128]{4,3,2,1,0:T(8,128)}, u32[]{:S(2)}, u32[]{:S(2)}) collective-permute-start(f32[2,2,1,256,128]{4,3,2,1,0:T(8,128)} %get-tuple-element.654), channel_id=1, source_target_pairs={{0,1},{1,2},{2,3},{3,4},{4,5},{5,6},{6,7},{7,8},{8,9},{9,10},{10,1... | collective-permute-start | bytes 1572872 | tf_op jit(solution)/shard_map/while/body/eval_jaxpr/ppermute | solution.py:26
  274.9 13.7 %collective-permute-start = (f32[2,2,1,256,128]{4,3,2,1,0:T(8,128)}, f32[2,2,1,256,128]{4,3,2,1,0:T(8,128)}, u32[]{:S(2)}, u32[]{:S(2)}) collective-permute-start(f32[2,2,1,256,128]{4,3,2,1,0:T(8,128)} %get-tuple-element.653), channel_id=1, source_target_pairs={{1,0},{2,1},{3,2},{4,3},{5,4},{6,5},{7,6},{8,7},{9,8},{10,9},{11,1... | collective-permute-start | bytes 1572872 | tf_op jit(solution)/shard_map/while/body/eval_jaxpr/ppermute | solution.py:29
  276.8 12.9 %collective-permute-start.1 = (f32[2,2,1,256,128]{4,3,2,1,0:T(8,128)}, f32[2,2,1,256,128]{4,3,2,1,0:T(8,128)}, u32[]{:S(2)}, u32[]{:S(2)}) collective-permute-start(f32[2,2,1,256,128]{4,3,2,1,0:T(8,128)} %get-tuple-element.654), channel_id=1, source_target_pairs={{0,1},{1,2},{2,3},{3,4},{4,5},{5,6},{6,7},{7,8},{8,9},{9,10},{10,1... | collective-permute-start | bytes 1572872 | tf_op jit(solution)/shard_map/while/body/eval_jaxpr/ppermute | solution.py:26
  295.8 13.7 %collective-permute-start = (f32[2,2,1,256,128]{4,3,2,1,0:T(8,128)}, f32[2,2,1,256,128]{4,3,2,1,0:T(8,128)}, u32[]{:S(2)}, u32[]{:S(2)}) collective-permute-start(f32[2,2,1,256,128]{4,3,2,1,0:T(8,128)} %get-tuple-element.653), channel_id=1, source_target_pairs={{1,0},{2,1},{3,2},{4,3},{5,4},{6,5},{7,6},{8,7},{9,8},{10,9},{11,1... | collective-permute-start | bytes 1572872 | tf_op jit(solution)/shard_map/while/body/eval_jaxpr/ppermute | solution.py:29
  297.7 12.9 %collective-permute-start.1 = (f32[2,2,1,256,128]{4,3,2,1,0:T(8,128)}, f32[2,2,1,256,128]{4,3,2,1,0:T(8,128)}, u32[]{:S(2)}, u32[]{:S(2)}) collective-permute-start(f32[2,2,1,256,128]{4,3,2,1,0:T(8,128)} %get-tuple-element.654), channel_id=1, source_target_pairs={{0,1},{1,2},{2,3},{3,4},{4,5},{5,6},{6,7},{7,8},{8,9},{9,10},{10,1... | collective-permute-start | bytes 1572872 | tf_op jit(solution)/shard_map/while/body/eval_jaxpr/ppermute | solution.py:26
  307.1 3.5 copy-start.2
  316.6 13.7 %collective-permute-start = (f32[2,2,1,256,128]{4,3,2,1,0:T(8,128)}, f32[2,2,1,256,128]{4,3,2,1,0:T(8,128)}, u32[]{:S(2)}, u32[]{:S(2)}) collective-permute-start(f32[2,2,1,256,128]{4,3,2,1,0:T(8,128)} %get-tuple-element.653), channel_id=1, source_target_pairs={{1,0},{2,1},{3,2},{4,3},{5,4},{6,5},{7,6},{8,7},{9,8},{10,9},{11,1... | collective-permute-start | bytes 1572872 | tf_op jit(solution)/shard_map/while/body/eval_jaxpr/ppermute | solution.py:29
  318.6 12.9 %collective-permute-start.1 = (f32[2,2,1,256,128]{4,3,2,1,0:T(8,128)}, f32[2,2,1,256,128]{4,3,2,1,0:T(8,128)}, u32[]{:S(2)}, u32[]{:S(2)}) collective-permute-start(f32[2,2,1,256,128]{4,3,2,1,0:T(8,128)} %get-tuple-element.654), channel_id=1, source_target_pairs={{0,1},{1,2},{2,3},{3,4},{4,5},{5,6},{6,7},{7,8},{8,9},{9,10},{10,1... | collective-permute-start | bytes 1572872 | tf_op jit(solution)/shard_map/while/body/eval_jaxpr/ppermute | solution.py:26
  328.0 3.5 copy-start.2
  337.5 13.7 %collective-permute-start = (f32[2,2,1,256,128]{4,3,2,1,0:T(8,128)}, f32[2,2,1,256,128]{4,3,2,1,0:T(8,128)}, u32[]{:S(2)}, u32[]{:S(2)}) collective-permute-start(f32[2,2,1,256,128]{4,3,2,1,0:T(8,128)} %get-tuple-element.653), channel_id=1, source_target_pairs={{1,0},{2,1},{3,2},{4,3},{5,4},{6,5},{7,6},{8,7},{9,8},{10,9},{11,1... | collective-permute-start | bytes 1572872 | tf_op jit(solution)/shard_map/while/body/eval_jaxpr/ppermute | solution.py:29
  339.4 12.9 %collective-permute-start.1 = (f32[2,2,1,256,128]{4,3,2,1,0:T(8,128)}, f32[2,2,1,256,128]{4,3,2,1,0:T(8,128)}, u32[]{:S(2)}, u32[]{:S(2)}) collective-permute-start(f32[2,2,1,256,128]{4,3,2,1,0:T(8,128)} %get-tuple-element.654), channel_id=1, source_target_pairs={{0,1},{1,2},{2,3},{3,4},{4,5},{5,6},{6,7},{7,8},{8,9},{9,10},{10,1... | collective-permute-start | bytes 1572872 | tf_op jit(solution)/shard_map/while/body/eval_jaxpr/ppermute | solution.py:26
  358.4 13.7 %collective-permute-start = (f32[2,2,1,256,128]{4,3,2,1,0:T(8,128)}, f32[2,2,1,256,128]{4,3,2,1,0:T(8,128)}, u32[]{:S(2)}, u32[]{:S(2)}) collective-permute-start(f32[2,2,1,256,128]{4,3,2,1,0:T(8,128)} %get-tuple-element.653), channel_id=1, source_target_pairs={{1,0},{2,1},{3,2},{4,3},{5,4},{6,5},{7,6},{8,7},{9,8},{10,9},{11,1... | collective-permute-start | bytes 1572872 | tf_op jit(solution)/shard_map/while/body/eval_jaxpr/ppermute | solution.py:29
  360.3 12.9 %collective-permute-start.1 = (f32[2,2,1,256,128]{4,3,2,1,0:T(8,128)}, f32[2,2,1,256,128]{4,3,2,1,0:T(8,128)}, u32[]{:S(2)}, u32[]{:S(2)}) collective-permute-start(f32[2,2,1,256,128]{4,3,2,1,0:T(8,128)} %get-tuple-element.654), channel_id=1, source_target_pairs={{0,1},{1,2},{2,3},{3,4},{4,5},{5,6},{6,7},{7,8},{8,9},{9,10},{10,1... | collective-permute-start | bytes 1572872 | tf_op jit(solution)/shard_map/while/body/eval_jaxpr/ppermute | solution.py:26
  379.3 13.7 %collective-permute-start = (f32[2,2,1,256,128]{4,3,2,1,0:T(8,128)}, f32[2,2,1,256,128]{4,3,2,1,0:T(8,128)}, u32[]{:S(2)}, u32[]{:S(2)}) collective-permute-start(f32[2,2,1,256,128]{4,3,2,1,0:T(8,128)} %get-tuple-element.653), channel_id=1, source_target_pairs={{1,0},{2,1},{3,2},{4,3},{5,4},{6,5},{7,6},{8,7},{9,8},{10,9},{11,1... | collective-permute-start | bytes 1572872 | tf_op jit(solution)/shard_map/while/body/eval_jaxpr/ppermute | solution.py:29
  381.2 12.9 %collective-permute-start.1 = (f32[2,2,1,256,128]{4,3,2,1,0:T(8,128)}, f32[2,2,1,256,128]{4,3,2,1,0:T(8,128)}, u32[]{:S(2)}, u32[]{:S(2)}) collective-permute-start(f32[2,2,1,256,128]{4,3,2,1,0:T(8,128)} %get-tuple-element.654), channel_id=1, source_target_pairs={{0,1},{1,2},{2,3},{3,4},{4,5},{5,6},{6,7},{7,8},{8,9},{9,10},{10,1... | collective-permute-start | bytes 1572872 | tf_op jit(solution)/shard_map/while/body/eval_jaxpr/ppermute | solution.py:26
  400.2 13.7 %collective-permute-start = (f32[2,2,1,256,128]{4,3,2,1,0:T(8,128)}, f32[2,2,1,256,128]{4,3,2,1,0:T(8,128)}, u32[]{:S(2)}, u32[]{:S(2)}) collective-permute-start(f32[2,2,1,256,128]{4,3,2,1,0:T(8,128)} %get-tuple-element.653), channel_id=1, source_target_pairs={{1,0},{2,1},{3,2},{4,3},{5,4},{6,5},{7,6},{8,7},{9,8},{10,9},{11,1... | collective-permute-start | bytes 1572872 | tf_op jit(solution)/shard_map/while/body/eval_jaxpr/ppermute | solution.py:29
  402.1 12.9 %collective-permute-start.1 = (f32[2,2,1,256,128]{4,3,2,1,0:T(8,128)}, f32[2,2,1,256,128]{4,3,2,1,0:T(8,128)}, u32[]{:S(2)}, u32[]{:S(2)}) collective-permute-start(f32[2,2,1,256,128]{4,3,2,1,0:T(8,128)} %get-tuple-element.654), channel_id=1, source_target_pairs={{0,1},{1,2},{2,3},{3,4},{4,5},{5,6},{6,7},{7,8},{8,9},{9,10},{10,1... | collective-permute-start | bytes 1572872 | tf_op jit(solution)/shard_map/while/body/eval_jaxpr/ppermute | solution.py:26
  421.0 13.7 %collective-permute-start = (f32[2,2,1,256,128]{4,3,2,1,0:T(8,128)}, f32[2,2,1,256,128]{4,3,2,1,0:T(8,128)}, u32[]{:S(2)}, u32[]{:S(2)}) collective-permute-start(f32[2,2,1,256,128]{4,3,2,1,0:T(8,128)} %get-tuple-element.653), channel_id=1, source_target_pairs={{1,0},{2,1},{3,2},{4,3},{5,4},{6,5},{7,6},{8,7},{9,8},{10,9},{11,1... | collective-permute-start | bytes 1572872 | tf_op jit(solution)/shard_map/while/body/eval_jaxpr/ppermute | solution.py:29
  422.9 12.9 %collective-permute-start.1 = (f32[2,2,1,256,128]{4,3,2,1,0:T(8,128)}, f32[2,2,1,256,128]{4,3,2,1,0:T(8,128)}, u32[]{:S(2)}, u32[]{:S(2)}) collective-permute-start(f32[2,2,1,256,128]{4,3,2,1,0:T(8,128)} %get-tuple-element.654), channel_id=1, source_target_pairs={{0,1},{1,2},{2,3},{3,4},{4,5},{5,6},{6,7},{7,8},{8,9},{9,10},{10,1... | collective-permute-start | bytes 1572872 | tf_op jit(solution)/shard_map/while/body/eval_jaxpr/ppermute | solution.py:26
  442.9 43.4 %collective-permute-start.8 = (f32[2,2,4,256,128]{4,3,2,0,1:T(8,128)}, f32[2,2,4,256,128]{4,3,2,0,1:T(8,128)}, u32[]{:S(2)}, u32[]{:S(2)}) collective-permute-start(f32[2,2,4,256,128]{4,3,2,0,1:T(8,128)} %maximum_bitcast_fusion.2), channel_id=1, source_target_pairs={{0,16},{16,0},{32,48},{48,32},{64,80},{80,64},{96,112},{112,96},{1... | collective-permute-start | bytes 6291464 | tf_op jit(solution)/shard_map/ppermute | solution.py:18
  487.0 3.9 copy-start.17
  490.9 46.0 %collective-permute-start.9 = (f32[2,2,4,256,128]{4,3,2,0,1:T(8,128)}, f32[2,2,4,256,128]{4,3,2,0,1:T(8,128)}, u32[]{:S(2)}, u32[]{:S(2)}) collective-permute-start(f32[2,2,4,256,128]{4,3,2,0,1:T(8,128)} %fusion.28), channel_id=1, source_target_pairs={{0,32},{16,48},{32,0},{48,16},{64,96},{80,112},{96,64},{112,80},{1... | collective-permute-start | bytes 6291464 | tf_op jit(solution)/shard_map/ppermute | solution.py:18
  545.4 46.9 %collective-permute-start.10 = (f32[2,2,4,256,128]{4,3,2,0,1:T(8,128)}, f32[2,2,4,256,128]{4,3,2,0,1:T(8,128)S(1)}, u32[]{:S(2)}, u32[]{:S(2)}) collective-permute-start(f32[2,2,4,256,128]{4,3,2,0,1:T(8,128)} %fusion.29), channel_id=1, source_target_pairs={{0,64},{16,80},{32,96},{48,112},{64,0},{80,16},{96,32},{112,48},{1... | collective-permute-start | bytes 6291464 | tf_op jit(solution)/shard_map/ppermute | solution.py:18
  (111 other events, 379.6 us)
where the time goes:
time: 599 us; the launch traced here: 598 us
  waiting for transfers between devices  325 us (54%)
  starting transfers between devices  116 us (19%)
  other arithmetic  93.9 us (16%)
  local copies, waits for them, and re-layouts  58.4 us (10%)
    ppermute x6, waiting for transfers between devices, swapped(): return lax.ppermute(value, axis, pairs)  275 us
    ppermute x13, starting transfers between devices, padded_2(): lax.ppermute(lax.slice_in_dim(block, block.shape[dim] - width, None, axis...  80.1 us
    sub x12, other arithmetic, operate(): return diag_sum * core - total  40.3 us
    slice x26, local copies, waits for them, and re-layouts, along(): lax.slice_in_dim(core, 0, length - 1, axis=axis)  40.1 us
    ppermute x13, waiting for transfers between devices, padded_2(): lax.ppermute(lax.slice_in_dim(block, 0, width, axis=dim), axis, backward)  28.4 us
    ppermute x13, starting transfers between devices, padded_2(): lax.ppermute(lax.slice_in_dim(block, 0, width, axis=dim), axis, backward)  25.7 us
    ppermute x13, waiting for transfers between devices, padded_2(): lax.ppermute(lax.slice_in_dim(block, block.shape[dim] - width, None, axis...  14.2 us
    slice x12, local copies, waits for them, and re-layouts, padded_2(): lax.slice_in_dim(block, block.shape[dim] - width, None, axis=dim)  13 us
  transfers between devices with their start and end apart: 33, of which 32 were waited for; matrix products, arithmetic and copies ran while one was open for 7% of the time, Pallas kernels for 0%

commit v1 on v0

v1 whole, which is shorter than its diff:
```python
import functools
import math

import jax
import jax.numpy as jnp
from jax import lax
from jax.experimental import pallas as pl
from jax.experimental.pallas import tpu as pltpu
from jax.sharding import PartitionSpec as P

SWEEPS = 12
MESH = pl.DeviceIdType.MESH
F32 = jnp.float32
OMEGAS = [
    1.0 / (1.0 + 0.7 * math.cos(math.pi * (2 * turn + 1) / (2 * SWEEPS))) for turn in range(SWEEPS)
]

TMS = 8
PL = 4
ROWS = 32
EP = PL + 4
ER = ROWS + 4
F = 16
R = 2
NPH = 16 // R
STEPS2 = SWEEPS // 2
TILE_ORDER = (0, 3, 1, 2)
PEERS = ((0, 1), (0, 3), (1, 0), (1, 1), (1, 3), (0, 2), (1, 2))


def real_dft(values):
    n = len(values)
    if n == 2:
        return [(values[0] + values[1], None), (values[0] - values[1], None)]
    even = real_dft(values[0::2])
    odd = real_dft(values[1::2])
    half = n // 2
    out = [None] * (half + 1)
    for k in range(half // 2 + 1):
        er, ei = even[k]
        orr, oi = odd[k]
        if k == 0:
            out[0] = (er + orr, None)
            out[half] = (er - orr, None)
        elif 2 * k == half:
            out[k] = (er, -orr)
        else:
            c, s = math.cos(2 * math.pi * k / n), -math.sin(2 * math.pi * k / n)
            if oi is None:
                tr, ti = orr * c, orr * s
            else:
                tr, ti = orr * c - oi * s, orr * s + oi * c
            out[k] = (er + tr, ti if ei is None else ei + ti)
            out[half - k] = (er - tr, ti if ei is None else ti - ei)
    return out


def real_sum(modes, n):
    if n == 2:
        return [modes[0][0] + modes[1][0], modes[0][0] - modes[1][0]]
    half = n // 2
    even, odd = [], []
    for k in range(half // 2 + 1):
        ar, ai = modes[k]
        br, bi = modes[half - k]
        if k == 0:
            even.append((ar + br, None))
            odd.append((ar - br, None))
        elif 2 * k == half:
            even.append((ar + ar, None))
            odd.append((-(ai + ai), None))
        else:
            c, s = math.cos(2 * math.pi * k / n), math.sin(2 * math.pi * k / n)
            even.append((ar + br, ai - bi))
            dr, di = ar - br, ai + bi
            odd.append((dr * c - di * s, dr * s + di * c))
    e = real_sum(even, half)
    o = real_sum(odd, half)
    out = [None] * n
    out[0::2] = e
    out[1::2] = o
    return out


def snake(p):
    return jnp.where(p < 4, p, 11 - p)


def pick(table, index):
    value = jnp.float32(table[0])
    for i in range(1, len(table)):
        value = jnp.where(index == i, jnp.float32(table[i]), value)
    return value


def kernel(
    ngx,
    state,
    start,
    kappa,
    weights,
    shift_real,
    shift_imag,
    out,
    w,
    wb,
    sb,
    stage,
    first,
    kst,
    tws,
    shifts,
    fx,
    fy,
    fzl,
    fzu,
    dg,
    ia,
    ib,
    ic,
    loc,
    a_s,
    a_r,
    t_s,
    t_r,
    k_s,
    k_r,
    h_s,
    h_r,
    hy_s,
    hy_r,
    x_s,
    x_r,
    y_s,
    y_r,
    c_s,
    c_r,
    o_s,
    o_r,
    o_l,
):
    tm = lax.axis_index("tm")
    gx = lax.axis_index("gx")
    p = snake(tm)
    zh = tm // 4
    xx = lax.rem(tm, 4)
    peers = [lax.rem(zh + dz, 2) * 4 + lax.rem(xx + dx, 4) for dz, dx in PEERS]
    has_lo, has_hi = gx > 0, gx < ngx - 1
    has_dn, has_up = p > 0, p < TMS - 1
    gxs = (gx - 1, gx + 1)
    tms = (snake(p - 1), snake(p + 1))
    x_to = (has_lo, has_hi)
    x_from = (has_hi, has_lo)
    y_to = (has_dn, has_up)
    y_from = (has_up, has_dn)
    row0 = pl.multiple_of(p * ROWS, ROWS)

    barrier = pltpu.get_barrier_semaphore()
    for peer in peers:
        pl.semaphore_signal(barrier, inc=1, device_id=(peer, gx), device_id_type=MESH)
    for d in range(2):

        @pl.when(x_to[d])
        def _():
            pl.semaphore_signal(barrier, inc=1, device_id=(tm, gxs[d]), device_id_type=MESH)

        for e in range(2):

            @pl.when(x_to[d] & y_to[e])
            def _():
                pl.semaphore_signal(
                    barrier, inc=1, device_id=(tms[e], gxs[d]), device_id_type=MESH
                )

    nx = has_lo.astype(jnp.int32) + has_hi.astype(jnp.int32)
    ny = has_dn.astype(jnp.int32) + has_up.astype(jnp.int32)

    own = [
        pltpu.make_async_copy(
            state.at[:, :, pl.ds(row0, ROWS)], stage.at[pl.ds(2 * tm, 2)], loc.at[0]
        ),
        pltpu.make_async_copy(start.at[:, pl.ds(row0, ROWS)], first, loc.at[1]),
    ]
    for copy in own:
        copy.start()
    pieces = (
        (None, row0, 8, ROWS),
        (has_dn, pl.multiple_of(jnp.maximum(row0 - 8, 0), 8), 0, 8),
        (has_up, pl.multiple_of(jnp.minimum(row0 + ROWS, (TMS - 1) * ROWS), 8), 8 + ROWS, 8),
    )

    def guarded(condition, body):
        if condition is None:
            body()
        else:
            pl.when(condition)(body)

    def kappa_own(i):
        _, r, at, n = pieces[i]
        return pltpu.make_async_copy(
            kappa.at[:, pl.ds(r, n)], kst.at[pl.ds(2, PL), pl.ds(at, n)], loc.at[2 + i]
        )

    def kappa_out(d, i):
        _, r, at, n = pieces[i]
        return pltpu.make_async_remote_copy(
            kappa.at[pl.ds(2 * d, 2), pl.ds(r, n)],
            kst.at[pl.ds(6 if d == 0 else 0, 2), pl.ds(at, n)],
            k_s.at[d, i],
            k_r.at[d, i],
            device_id=(tm, gxs[d]),
            device_id_type=MESH,
        )

    for i in range(3):
        guarded(pieces[i][0], lambda i=i: kappa_own(i).start())

    for i in range(2):
        tws[2 * tm + i] = jnp.full((8, 128), weights[i], F32)

    pl.semaphore_wait(barrier, 7 + nx + nx * ny)

    def tile_out(j, tile):
        rows = pl.multiple_of(snake(peers[j]) * ROWS + 8 * tile, 8)
        return pltpu.make_async_remote_copy(
            state.at[:, :, pl.ds(rows, 8)],
            stage.at[pl.ds(2 * tm, 2), :, pl.ds(8 * tile, 8)],
            a_s.at[j, tile],
            a_r.at[j, tile],
            device_id=(peers[j], gx),
            device_id_type=MESH,
        )

    def weight_out(j):
        return pltpu.make_async_remote_copy(
            tws.at[pl.ds(2 * tm, 2)],
            tws.at[pl.ds(2 * tm, 2)],
            t_s.at[j],
            t_r.at[j],
            device_id=(peers[j], gx),
            device_id_type=MESH,
        )

    for d in range(2):
        for i in range(3):
            condition = x_to[d] if pieces[i][0] is None else x_to[d] & pieces[i][0]
            guarded(condition, lambda d=d, i=i: kappa_out(d, i).start())
    for j in range(7):
        weight_out(j).start()
    for tile in TILE_ORDER:
        for j in range(7):
            tile_out(j, tile).start()

    def clear_planes(ref, base, at):
        def body(r, _):
            for i in range(2):
                ref[base + at + i, pl.ds(pl.multiple_of(r * 64, 64), 64)] = jnp.zeros((64, 128), F32)
            return 0

        lax.fori_loop(0, ER * F // 64, body, 0)

    def clear_rows(ref, base, at):
        def body(i, _):
            ref[base + i, pl.ds(at * F, 2 * F)] = jnp.zeros((2 * F, 128), F32)
            return 0

        lax.fori_loop(0, EP, body, 0)

    def clear(condition, planes, at):
        @pl.when(condition)
        def _():
            for i in range(3):
                (clear_planes if planes else clear_rows)(w, i * EP, at)
            (clear_planes if planes else clear_rows)(sb, 0, at)

    clear(gx == 0, True, 0)
    clear(gx == ngx - 1, True, EP - 2)
    clear(p == 0, False, 0)
    clear(p == TMS - 1, False, ER - 2)
    for condition, at in ((gx == 0, 0), (gx == ngx - 1, EP - 2)):

        @pl.when(condition)
        def _():
            kst[pl.ds(at, 2)] = jnp.zeros((2, ROWS + 16, 128), F32)

    for condition, at in ((p == 0, 0), (p == TMS - 1, 8 + ROWS)):

        @pl.when(condition)
        def _():
            kst[:, pl.ds(at, 8)] = jnp.zeros((EP, 8, 128), F32)

    lane = lax.broadcasted_iota(jnp.int32, (8, 128), 1)
    sub = lax.broadcasted_iota(jnp.int32, (8, 128), 0)
    s_a = jnp.full((8, 128), shift_real[0], F32)
    s_c = jnp.full((8, 128), shift_real[8], F32)
    s_i = jnp.zeros((8, 128), F32)
    for m in range(1, 8):
        s_a = jnp.where(sub == m, shift_real[m], s_a)
        s_c = jnp.where(sub == m, shift_real[m], s_c)
        s_i = jnp.where(sub == m, shift_imag[m], s_i)
    shifts[0] = s_a
    shifts[1] = s_c
    shifts[2] = s_i

    for i in range(3):
        guarded(pieces[i][0], lambda i=i: kappa_own(i).wait())
    for d in range(2):
        for i in range(3):
            cond_from = x_from[d] if pieces[i][0] is None else x_from[d] & pieces[i][0]
            cond_to = x_to[d] if pieces[i][0] is None else x_to[d] & pieces[i][0]
            guarded(cond_from, lambda d=d, i=i: kappa_out(d, i).wait_recv())
            guarded(cond_to, lambda d=d, i=i: kappa_out(d, i).wait_send())

    def coefficients(yi, _):
        at = pl.multiple_of(yi * 8, 8)

        def cell(px, dy):
            return jnp.broadcast_to(kst[px, pl.ds(yi + 6 + dy, 1), :], (8, 128))

        s_a, s_c, s_i = shifts[0], shifts[1], shifts[2]
        outside_y = ((p == 0) & (yi < 2)) | ((p == TMS - 1) & (yi > ER - 3))
        below, here = cell(0, 0), cell(1, 0)
        low = 0.5 * (here + below)
        for px in range(1, EP - 1):
            above = cell(px + 1, 0)
            high = 0.5 * (here + above)
            yl = 0.5 * (here + cell(px, -1))
            yu = 0.5 * (here + cell(px, 1))
            k_low = jnp.where(lane == 0, 0.0, pltpu.roll(here, 1, 1))
            k_high = jnp.where(lane == 127, 0.0, pltpu.roll(here, 127, 1))
            zl = 0.5 * (here + k_low)
            zu = 0.5 * (here + k_high)
            diag = low + high + yl + yu + zl + zu
            fx[px, pl.ds(at, 8)] = low
            if px == EP - 2:
                fx[px + 1, pl.ds(at, 8)] = high
            fy[px, pl.ds(at, 8)] = yl
            fy[px, pl.ds(pl.multiple_of(at + 8, 8), 8)] = yu
            fzl[px, pl.ds(at, 8)] = jnp.where(lane == 0, 0.0, zl)
            fzu[px, pl.ds(at, 8)] = jnp.where(lane == 127, 0.0, zu)
            dg[px, pl.ds(at, 8)] = diag
            outside = outside_y
            if px == 1:
                outside = outside | (gx == 0)
            if px == EP - 2:
                outside = outside | (gx == ngx - 1)
            inside = jnp.where(outside, 0.0, 1.0).astype(F32)
            d_a = s_a + diag
            ratio = inside / (d_a * d_a + s_i * s_i)
            ia[px, pl.ds(at, 8)] = d_a * ratio
            ib[px, pl.ds(at, 8)] = -s_i * ratio
            d_c = s_c + diag
            ic[px, pl.ds(at, 8)] = d_c * (inside / (d_c * d_c + s_i * s_i))
            here, low = above, high
        return 0

    lax.fori_loop(1, ER - 1, coefficients, 0)

    def forward(tile):
        rows = pl.multiple_of(tile * 8, 8)

        def plane(x, _):
            base = (8 * tile + 2) * F

            def put(ref, at, modes):
                for m in range(9):
                    re, im = modes[m]
                    if m == 8:
                        ref[at, pl.ds(base + 8, 8, stride=F), :] = re
                        continue
                    ref[at, pl.ds(base + m, 8, stride=F), :] = re
                    if m > 0:
                        ref[at, pl.ds(base + 8 + m, 8, stride=F), :] = im

            now = [stage[t, x, pl.ds(rows, 8), :] for t in range(16)]
            put(sb, x + 2, real_dft([tws[t] * now[t] for t in range(16)]))
            before = [first[x, pl.ds(rows, 8), :]] + now[:15]
            put(
                w,
                x + 2,
                real_dft([tws[t] * (before[t] - now[t] * now[t] * now[t]) for t in range(16)]),
            )
            return 0

        lax.fori_loop(0, PL, plane, 0)

    def h_copy(d, tile):
        rows = pl.ds(pl.multiple_of((8 * tile + 2) * F, 8), 8 * F)
        return pltpu.make_async_remote_copy(
            sb.at[2 if d == 0 else EP - 3, rows],
            sb.at[EP - 2 if d == 0 else 1, rows],
            h_s.at[d, tile],
            h_r.at[d, tile],
            device_id=(tm, gxs[d]),
            device_id_type=MESH,
        )

    def hy_copy(d):
        return pltpu.make_async_remote_copy(
            sb.at[pl.ds(2, PL), pl.ds((2 if d == 0 else ER - 3) * F, F)],
            sb.at[pl.ds(2, PL), pl.ds((ER - 2 if d == 0 else 1) * F, F)],
            hy_s.at[d],
            hy_r.at[d],
            device_id=(tms[d], gx),
            device_id_type=MESH,
        )

    def x_copy(buf, par, d, e, i):
        r = R * i if e == 0 else ROWS - R - R * i
        rows = pl.ds(pl.multiple_of((r + 2) * F, 8), R * F)
        return pltpu.make_async_remote_copy(
            w.at[pl.ds(buf + (2 if d == 0 else EP - 4), 2), rows],
            w.at[pl.ds(buf + (EP - 2 if d == 0 else 0), 2), rows],
            x_s.at[d, e, i],
            x_r.at[par, d, e, i],
            device_id=(tm, gxs[d]),
            device_id_type=MESH,
        )

    def y_copy(buf, par, d):
        return pltpu.make_async_remote_copy(
            w.at[pl.ds(buf + 2, PL), pl.ds((2 if d == 0 else ER - 4) * F, 2 * F)],
            w.at[pl.ds(buf + 2, PL), pl.ds((ER - 2 if d == 0 else 0) * F, 2 * F)],
            y_s.at[d],
            y_r.at[par, d],
            device_id=(tms[d], gx),
            device_id_type=MESH,
        )

    def c_copy(buf, par, d, e):
        return pltpu.make_async_remote_copy(
            w.at[buf + (2 if d == 0 else EP - 3), pl.ds((2 if e == 0 else ER - 3) * F, F)],
            w.at[buf + (EP - 2 if d == 0 else 1), pl.ds((ER - 2 if e == 0 else 1) * F, F)],
            c_s.at[d, e],
            c_r.at[par, d, e],
            device_id=(tms[e], gxs[d]),
            device_id_type=MESH,
        )

    def x_start(buf, par, i):
        for e in range(2):
            for d in range(2):
                pl.when(x_to[d])(lambda d=d, e=e: x_copy(buf, par, d, e, i).start())

    def x_wait_send(buf, par, i):
        for e in range(2):
            for d in range(2):
                pl.when(x_to[d])(lambda d=d, e=e: x_copy(buf, par, d, e, i).wait_send())

    def x_wait_recv(buf, par, i):
        for e in range(2):
            for d in range(2):
                pl.when(x_from[d])(lambda d=d, e=e: x_copy(buf, par, d, e, i).wait_recv())

    def edges_start(buf, par):
        for d in range(2):
            pl.when(y_to[d])(lambda d=d: y_copy(buf, par, d).start())
        for d in range(2):
            for e in range(2):
                pl.when(x_to[d] & y_to[e])(lambda d=d, e=e: c_copy(buf, par, d, e).start())

    def edges_wait_send(buf, par):
        for d in range(2):
            pl.when(y_to[d])(lambda d=d: y_copy(buf, par, d).wait_send())
        for d in range(2):
            for e in range(2):
                pl.when(x_to[d] & y_to[e])(lambda d=d, e=e: c_copy(buf, par, d, e).wait_send())

    def edges_wait_recv(buf, par):
        for d in range(2):
            pl.when(y_from[d])(lambda d=d: y_copy(buf, par, d).wait_recv())
        for d in range(2):
            for e in range(2):
                pl.when(x_from[d] & y_from[e])(
                    lambda d=d, e=e: c_copy(buf, par, d, e).wait_recv()
                )

    def row_parts(ref, base, yi, low, high):
        at = pl.multiple_of(yi * 8, 8)
        rows = [pl.multiple_of(yi * F + 8 * t, 8) for t in range(2)]

        def get(px, t, dy):
            return ref[base + px, pl.ds(pl.multiple_of(rows[t] + dy * F, 8), 8), :]

        below = [get(low - 1, t, 0) for t in range(2)]
        here = [get(low, t, 0) for t in range(2)]
        face_low = fx[low, pl.ds(at, 8)]
        for px in range(low, high):
            face_high = fx[px + 1, pl.ds(at, 8)]
            y_low = fy[px, pl.ds(at, 8)]
            y_high = fy[px, pl.ds(pl.multiple_of(at + 8, 8), 8)]
            z_low = fzl[px, pl.ds(at, 8)]
            z_high = fzu[px, pl.ds(at, 8)]
            sums = []
            above = []
            for t in range(2):
                up = get(px + 1, t, 0)
                above.append(up)
                total = face_low * below[t] + face_high * up
                total = total + (y_low * get(px, t, -1) + y_high * get(px, t, 1))
                total = total + (
                    z_low * pltpu.roll(here[t], 1, 1) + z_high * pltpu.roll(here[t], 127, 1)
                )
                sums.append(total)
            yield px, at, rows, here, sums
            below, here, face_low = here, above, face_high

    def divided(px, at, value):
        a, b, c = ia[px, pl.ds(at, 8)], ib[px, pl.ds(at, 8)], ic[px, pl.ds(at, 8)]
        return [a * value[0] - b * value[1], c * value[1] + b * value[0]]

    def starts(yi):
        results = []
        for px, at, rows, here, sums in row_parts(sb, 0, yi, 2, EP - 2):
            diag = dg[px, pl.ds(at, 8)]
            right = [
                w[px, pl.ds(rows[t], 8), :] - (diag * here[t] - sums[t]) for t in range(2)
            ]
            results.append((px, rows, divided(px, at, right)))
        for px, rows, value in results:
            for t in range(2):
                w[px, pl.ds(rows[t], 8), :] = value[t]

    def sweep(ref, base, target, target_base, yi, low, high, omega):
        results = []
        for px, at, rows, here, sums in row_parts(ref, base, yi, low, high):
            step = divided(px, at, sums)
            new = [
                (1.0 - omega) * here[t] + omega * (w[px, pl.ds(rows[t], 8), :] + step[t])
                for t in range(2)
            ]
            results.append((px, rows, new))
        for px, rows, value in results:
            for t in range(2):
                target[target_base + px, pl.ds(rows[t], 8), :] = value[t]

    def over(begin, count, body):
        def each(r, _):
            body(begin + r + 2)
            return 0

        lax.fori_loop(0, count, each, 0)

    def start_phase(i):
        over(R * i, R, starts)
        over(ROWS - R - R * i, R, starts)
        x_start(0, 0, i)

    for copy in own:
        copy.wait()
    for j in range(7):
        weight_out(j).wait_recv()
    for tiles in (TILE_ORDER[:2], TILE_ORDER[2:]):
        for tile in tiles:
            for j in range(7):
                tile_out(j, tile).wait_recv()
            forward(tile)
            for d in range(2):
                pl.when(x_to[d])(lambda d=d, tile=tile: h_copy(d, tile).start())
            if tile == 0:
                pl.when(y_to[0])(lambda: hy_copy(0).start())
            if tile == 3:
                pl.when(y_to[1])(lambda: hy_copy(1).start())
    for tiles in (TILE_ORDER[:2], TILE_ORDER[2:]):
        for tile in tiles:
            for d in range(2):
                pl.when(x_from[d])(lambda d=d, tile=tile: h_copy(d, tile).wait_recv())
            if tile == 0:
                pl.when(y_from[1])(lambda: hy_copy(1).wait_recv())
            if tile == 3:
                pl.when(y_from[0])(lambda: hy_copy(0).wait_recv())
        if tiles[0] == 0:
            start_phase(0)
            edges_start(0, 0)
            lax.fori_loop(1, NPH // 2, lambda i, _: (start_phase(i), 0)[1], 0)
        else:
            lax.fori_loop(NPH // 2, NPH, lambda i, _: (start_phase(i), 0)[1], 0)
    for tile in range(4):
        for d in range(2):
            pl.when(x_to[d])(lambda d=d, tile=tile: h_copy(d, tile).wait_send())
    for d in range(2):
        pl.when(y_to[d])(lambda d=d: hy_copy(d).wait_send())

    def home(tile, j):
        return pltpu.make_async_remote_copy(
            stage.at[pl.ds(2 * peers[j], 2), :, pl.ds(pl.multiple_of(8 * tile, 8), 8)],
            out.at[:, :, pl.ds(pl.multiple_of(row0 + 8 * tile, 8), 8)],
            o_s.at[j, tile],
            o_r.at[j, tile],
            device_id=(peers[j], gx),
            device_id_type=MESH,
        )

    def home_recv(tile, j):
        return pltpu.make_async_remote_copy(
            stage.at[pl.ds(2 * tm, 2), :, pl.ds(pl.multiple_of(8 * tile, 8), 8)],
            out.at[:, :, pl.ds(pl.multiple_of(snake(peers[j]) * ROWS + 8 * tile, 8), 8)],
            o_s.at[j, tile],
            o_r.at[j, tile],
            device_id=(peers[j], gx),
            device_id_type=MESH,
        )

    def home_own(tile):
        return pltpu.make_async_copy(
            stage.at[pl.ds(2 * tm, 2), :, pl.ds(pl.multiple_of(8 * tile, 8), 8)],
            out.at[:, :, pl.ds(pl.multiple_of(row0 + 8 * tile, 8), 8)],
            o_l.at[tile],
        )

    def backward(buf, tile):
        rows = pl.multiple_of(tile * 8, 8)

        def plane(x, _):
            base = (8 * tile + 2) * F
            field = [w[buf + x + 2, pl.ds(base + f, 8, stride=F), :] for f in range(F)]
            modes = [(field[0], None)]
            modes += [(field[m], field[8 + m]) for m in range(1, 8)]
            modes += [(field[8], None)]
            back = real_sum(modes, 16)
            for t in range(16):
                stage[t, x, pl.ds(rows, 8), :] = stage[t, x, pl.ds(rows, 8), :] + back[t] / (
                    16.0 * tws[t]
                )
            return 0

        lax.fori_loop(0, PL, plane, 0)
        for j in range(7):
            home(tile, j).start()
        home_own(tile).start()

    def two_sweeps(k, _):
        par = lax.rem(k, 2)
        source = jnp.where(k == 0, 0, (1 + par) * EP)
        result = (2 - par) * EP
        om_a = pick(OMEGAS[0::2], k)
        om_b = pick(OMEGAS[1::2], k)

        def first_sweep(begin, count):
            over(begin, count, lambda yi: sweep(w, source, wb, 0, yi, 1, EP - 1, om_a))

        def second_sweep(begin, count):
            over(begin, count, lambda yi: sweep(wb, 0, w, result, yi, 2, EP - 2, om_b))

        def pass_on(i):
            x_wait_send(result, par, i)

            @pl.when(k < STEPS2 - 1)
            def _():
                x_start(result, 1 - par, i)

        def finish(i):
            @pl.when(k == STEPS2 - 1)
            def _():
                backward(result, i)
                backward(result, 3 - i)

        edges_wait_recv(source, par)
        x_wait_recv(source, par, 0)
        x_wait_recv(source, par, 1)
        first_sweep(-1, R + 2)
        first_sweep(ROWS - 1 - R, R + 2)
        second_sweep(0, R)
        second_sweep(ROWS - R, R)
        pass_on(0)
        edges_wait_send(result, par)

        @pl.when(k < STEPS2 - 1)
        def _():
            edges_start(result, 1 - par)

        def phase(i, _):
            x_wait_recv(source, par, i + 1)
            first_sweep(R * i + 1, R)
            first_sweep(ROWS - 1 - R - R * i, R)
            second_sweep(R * i, R)
            second_sweep(ROWS - R - R * i, R)
            pass_on(i)

            @pl.when(i == NPH // 2 - 1)
            def _():
                finish(0)

            return 0

        lax.fori_loop(1, NPH - 1, phase, 0)
        first_sweep(17 - R, 2 * R - 2)
        second_sweep(16 - R, 2 * R)
        pass_on(NPH - 1)
        finish(1)
        return 0

    lax.fori_loop(0, STEPS2, two_sweeps, 0)

    for j in range(7):
        weight_out(j).wait_send()
        for tile in range(4):
            tile_out(j, tile).wait_send()
    for tile in TILE_ORDER:
        home_own(tile).wait()
        for j in range(7):
            home(tile, j).wait_send()
            home_recv(tile, j).wait_recv()


def shards(ngx, state, start_field, diffusivity, time_weights, shift_real, shift_imag):
    dma = pltpu.SemaphoreType.DMA
    any_space = pl.BlockSpec(memory_space=pl.ANY)
    smem = pl.BlockSpec(memory_space=pltpu.SMEM)
    coefficient = pltpu.VMEM((EP, ER * 8, 128), F32)
    return pl.pallas_call(
        functools.partial(kernel, ngx),
        out_shape=jax.ShapeDtypeStruct(state.shape, F32),
        in_specs=[any_space, any_space, any_space, smem, smem, smem],
        out_specs=any_space,
        scratch_shapes=[
            pltpu.VMEM((3 * EP, ER * F, 128), F32),
            pltpu.VMEM((EP, ER * F, 128), F32),
            pltpu.VMEM((EP, ER * F, 128), F32),
            pltpu.VMEM((16, PL, ROWS, 128), F32),
            pltpu.VMEM((PL, ROWS, 128), F32),
            pltpu.VMEM((EP, ROWS + 16, 128), F32),
            pltpu.VMEM((16, 8, 128), F32),
            pltpu.VMEM((3, 8, 128), F32),
        ]
        + [coefficient] * 8
        + [
            dma((5,)),
            dma((7, 4)),
            dma((7, 4)),
            dma((7,)),
            dma((7,)),
            dma((2, 3)),
            dma((2, 3)),
            dma((2, 4)),
            dma((2, 4)),
            dma((2,)),
            dma((2,)),
            dma((2, 2, NPH)),
            dma((2, 2, 2, NPH)),
            dma((2,)),
            dma((2, 2)),
            dma((2, 2)),
            dma((2, 2, 2)),
            dma((7, 4)),
            dma((7, 4)),
            dma((4,)),
        ],
        compiler_params=pltpu.CompilerParams(
            collective_id=0, has_side_effects=True, vmem_limit_bytes=44 * 2**20
        ),
        cost_estimate=pl.CostEstimate(
            flops=200_000_000, bytes_accessed=4 * 2**20, transcendentals=0
        ),
    )(state, start_field, diffusivity, time_weights, shift_real, shift_imag)


def solution(mesh):
    in_specs = (
        P("tm", "gx", None, None),
        P("gx", None, None),
        P("gx", None, None),
        P("tm"),
        P(),
        P(),
    )
    return jax.shard_map(
        functools.partial(shards, mesh.shape["gx"]),
        mesh=mesh,
        in_specs=in_specs,
        out_specs=P("tm", "gx", None, None),
        check_vma=False,
    )
```

time: 599 us -> 113 us (0.19)
  the two profiles are of different devices: /device:TPU:91 before, /device:TPU:1 now
where the time goes in v1:
time: 113 us
  Pallas kernels  107 us (95%)
  local copies, waits for them, and re-layouts  6.24 us (6%)
    pallas_call x1, Pallas kernels, shards(): pl.pallas_call(functools.partial(kernel, ngx), out_shape=jax.ShapeDtypeSt...  107 us
    unnamed x13, local copies, waits for them, and re-layouts  6.24 us

profile of v1, /device:TPU:1, one launch (start us, length us, event | category | flops | bytes accessed | tf_op | source)
XLA Modules:
  0.0 112.8 jit_solution(12167112331277178957)
XLA Ops:
  0.0 0.0 copy-start
  0.0 1.2 %copy-done = f32[2,4,256,128]{3,2,1,0:T(8,128)S(1)} copy-done((f32[2,4,256,128]{3,2,1,0:T(8,128)S(1)}, f32[2,4,256,128]{3,2,1,0:T(8,128)}, u32[]{:S(2)}) %copy-start) | copy-done | bytes 1048600
  1.2 0.0 copy-start.1
  1.2 1.0 copy-done.1
  2.3 0.0 copy-start.2
  2.3 1.0 copy-done.2
  3.3 0.0 copy-start.3
  3.3 0.7 copy-done.3
  4.0 0.0 copy-start.4
  4.0 0.7 copy-done.4
  4.6 0.0 copy-start.5
  4.6 0.7 copy-done.5
  5.3 106.6 %shard_map.64 = f32[2,4,256,128]{3,2,1,0:T(8,128)S(1)} custom-call(f32[2,4,256,128]{3,2,1,0:T(8,128)S(1)} %copy-done, f32[4,256,128]{2,1,0:T(8,128)S(1)} %copy-done.1, f32[4,256,128]{2,1,0:T(8,128)S(1)} %copy-done.2, f32[2]{0:T(128)S(1)} %copy-done.3, f32[16]{0:T(128)S(1)} %copy-done.4, f32[16]{0:T(128)S(1)} %copy-done.5), custom_call_target="tpu_custom_call" | custom-call | flops 200000000 | bytes 4194304 | tf_op jit(solution)/shard_map/pallas_call | solution.py:711
  111.9 1.0 copy.8
Async XLA Ops:
  0.0 1.2 %copy-start = (f32[2,4,256,128]{3,2,1,0:T(8,128)S(1)}, f32[2,4,256,128]{3,2,1,0:T(8,128)}, u32[]{:S(2)}) copy-start(f32[2,4,256,128]{3,2,1,0:T(8,128)} %state.1) | copy-start | bytes 3145732
  1.2 1.0 copy-start.1
  2.3 1.0 copy-start.2
  3.3 0.7 copy-start.3
  4.0 0.7 copy-start.4
  4.6 0.7 copy-start.5

commit v2 on v1

--- a/solution.py
+++ b/solution.py
@@ -18,12 +18,13 @@
 TMS = 8
 PL = 4
 ROWS = 32
-EP = PL + 4
-ER = ROWS + 4
+H = 3
+EP = PL + 2 * H
+ER = ROWS + 2 * H
 F = 16
-R = 2
+R = 4
 NPH = 16 // R
-STEPS2 = SWEEPS // 2
+STEPS = SWEEPS // H
 TILE_ORDER = (0, 3, 1, 2)
 PEERS = ((0, 1), (0, 3), (1, 0), (1, 1), (1, 3), (0, 2), (1, 2))
 
@@ -98,11 +99,15 @@
     state,
     start,
     kappa,
+    weights_in,
+    shift_real_in,
+    shift_imag_in,
+    out,
     weights,
     shift_real,
     shift_imag,
-    out,
     w,
+    w0,
     wb,
     sb,
     stage,
@@ -138,6 +143,10 @@
     o_s,
     o_r,
     o_l,
+    passing,
+    passing_row,
+    p_s,
+    p_r,
 ):
     tm = lax.axis_index("tm")
     gx = lax.axis_index("gx")
@@ -155,6 +164,21 @@
     y_from = (has_up, has_dn)
     row0 = pl.multiple_of(p * ROWS, ROWS)
 
+    turning = (tm == 3) | (tm == 7)
+    side = jnp.where(gx < ngx // 2, gx + ngx // 2, gx - ngx // 2)
+    side_pair = side + 1 - 2 * lax.rem(side, 2)
+    at_end = (gx < 2) | (gx >= ngx - 2)
+    relayed = tuple(at_end & (tm == turn) for turn in (7, 3))
+    relaying = tuple((gx >= ngx // 2 - 2) & (gx < ngx // 2 + 2) & (tm == turn) for turn in (3, 7))
+    even = lax.rem(gx, 2) == 0
+    c_to = [
+        [
+            x_to[d] & y_to[e] & jnp.logical_not(relayed[e] & (even if d == 1 else ~even))
+            for e in range(2)
+        ]
+        for d in range(2)
+    ]
+
     barrier = pltpu.get_barrier_semaphore()
     for peer in peers:
         pl.semaphore_signal(barrier, inc=1, device_id=(peer, gx), device_id_type=MESH)
@@ -171,6 +195,13 @@
                 pl.semaphore_signal(
                     barrier, inc=1, device_id=(tms[e], gxs[d]), device_id_type=MESH
                 )
+
+    in_relay = turning & (at_end | ((gx >= ngx // 2 - 2) & (gx < ngx // 2 + 2)))
+
+    @pl.when(in_relay)
+    def _():
+        for there in ((10 - tm, side), (tm, side), (tm, side_pair)):
+            pl.semaphore_signal(barrier, inc=1, device_id=there, device_id_type=MESH)
 
     nx = has_lo.astype(jnp.int32) + has_hi.astype(jnp.int32)
     ny = has_dn.astype(jnp.int32) + has_up.astype(jnp.int32)
@@ -181,7 +212,13 @@
         ),
         pltpu.make_async_copy(start.at[:, pl.ds(row0, ROWS)], first, loc.at[1]),
     ]
-    for copy in own:
+    scalars = [
+        pltpu.make_async_copy(source, target, loc.at[5 + i])
+        for i, (source, target) in enumerate(
+            ((weights_in, weights), (shift_real_in, shift_real), (shift_imag_in, shift_imag))
+        )
+    ]
+    for copy in scalars + own:
         copy.start()
     pieces = (
         (None, row0, 8, ROWS),
@@ -198,14 +235,14 @@
     def kappa_own(i):
         _, r, at, n = pieces[i]
         return pltpu.make_async_copy(
-            kappa.at[:, pl.ds(r, n)], kst.at[pl.ds(2, PL), pl.ds(at, n)], loc.at[2 + i]
+            kappa.at[:, pl.ds(r, n)], kst.at[pl.ds(H, PL), pl.ds(at, n)], loc.at[2 + i]
         )
 
     def kappa_out(d, i):
         _, r, at, n = pieces[i]
         return pltpu.make_async_remote_copy(
-            kappa.at[pl.ds(2 * d, 2), pl.ds(r, n)],
-            kst.at[pl.ds(6 if d == 0 else 0, 2), pl.ds(at, n)],
+            kappa.at[pl.ds(0 if d == 0 else PL - H, H), pl.ds(r, n)],
+            kst.at[pl.ds(EP - H if d == 0 else 0, H), pl.ds(at, n)],
             k_s.at[d, i],
             k_r.at[d, i],
             device_id=(tm, gxs[d]),
@@ -215,10 +252,7 @@
     for i in range(3):
         guarded(pieces[i][0], lambda i=i: kappa_own(i).start())
 
-    for i in range(2):
-        tws[2 * tm + i] = jnp.full((8, 128), weights[i], F32)
-
-    pl.semaphore_wait(barrier, 7 + nx + nx * ny)
+    pl.semaphore_wait(barrier, 7 + nx + nx * ny + 3 * in_relay.astype(jnp.int32))
 
     def tile_out(j, tile):
         rows = pl.multiple_of(snake(peers[j]) * ROWS + 8 * tile, 8)
@@ -245,23 +279,28 @@
         for i in range(3):
             condition = x_to[d] if pieces[i][0] is None else x_to[d] & pieces[i][0]
             guarded(condition, lambda d=d, i=i: kappa_out(d, i).start())
-    for j in range(7):
-        weight_out(j).start()
     for tile in TILE_ORDER:
         for j in range(7):
             tile_out(j, tile).start()
+        if tile == 0:
+            for copy in scalars:
+                copy.wait()
+            for i in range(2):
+                tws[2 * tm + i] = jnp.full((8, 128), weights[i], F32)
+            for j in range(7):
+                weight_out(j).start()
 
     def clear_planes(ref, base, at):
         def body(r, _):
-            for i in range(2):
-                ref[base + at + i, pl.ds(pl.multiple_of(r * 64, 64), 64)] = jnp.zeros((64, 128), F32)
+            for i in range(H):
+                ref[base + at + i, pl.ds(pl.multiple_of(r * 32, 32), 32)] = jnp.zeros((32, 128), F32)
             return 0
 
-        lax.fori_loop(0, ER * F // 64, body, 0)
+        lax.fori_loop(0, ER * F // 32, body, 0)
 
     def clear_rows(ref, base, at):
         def body(i, _):
-            ref[base + i, pl.ds(at * F, 2 * F)] = jnp.zeros((2 * F, 128), F32)
+            ref[base + i, pl.ds(at * F, H * F)] = jnp.zeros((H * F, 128), F32)
             return 0
 
         lax.fori_loop(0, EP, body, 0)
@@ -269,19 +308,20 @@
     def clear(condition, planes, at):
         @pl.when(condition)
         def _():
-            for i in range(3):
+            for i in range(2):
                 (clear_planes if planes else clear_rows)(w, i * EP, at)
+            (clear_planes if planes else clear_rows)(w0, 0, at)
             (clear_planes if planes else clear_rows)(sb, 0, at)
 
     clear(gx == 0, True, 0)
-    clear(gx == ngx - 1, True, EP - 2)
+    clear(gx == ngx - 1, True, EP - H)
     clear(p == 0, False, 0)
-    clear(p == TMS - 1, False, ER - 2)
-    for condition, at in ((gx == 0, 0), (gx == ngx - 1, EP - 2)):
+    clear(p == TMS - 1, False, ER - H)
+    for condition, at in ((gx == 0, 0), (gx == ngx - 1, EP - H)):
 
         @pl.when(condition)
         def _():
-            kst[pl.ds(at, 2)] = jnp.zeros((2, ROWS + 16, 128), F32)
+            kst[pl.ds(at, H)] = jnp.zeros((H, ROWS + 16, 128), F32)
 
     for condition, at in ((p == 0, 0), (p == TMS - 1, 8 + ROWS)):
 
@@ -315,10 +355,10 @@
         at = pl.multiple_of(yi * 8, 8)
 
         def cell(px, dy):
-            return jnp.broadcast_to(kst[px, pl.ds(yi + 6 + dy, 1), :], (8, 128))
+            return jnp.broadcast_to(kst[px, pl.ds(yi + 8 - H + dy, 1), :], (8, 128))
 
         s_a, s_c, s_i = shifts[0], shifts[1], shifts[2]
-        outside_y = ((p == 0) & (yi < 2)) | ((p == TMS - 1) & (yi > ER - 3))
+        outside_y = ((p == 0) & (yi < H)) | ((p == TMS - 1) & (yi > ER - 1 - H))
         below, here = cell(0, 0), cell(1, 0)
         low = 0.5 * (here + below)
         for px in range(1, EP - 1):
@@ -340,9 +380,9 @@
             fzu[px, pl.ds(at, 8)] = jnp.where(lane == 127, 0.0, zu)
             dg[px, pl.ds(at, 8)] = diag
             outside = outside_y
-            if px == 1:
+            if px < H:
                 outside = outside | (gx == 0)
-            if px == EP - 2:
+            if px > EP - 1 - H:
                 outside = outside | (gx == ngx - 1)
             inside = jnp.where(outside, 0.0, 1.0).astype(F32)
             d_a = s_a + diag
@@ -360,7 +400,7 @@
         rows = pl.multiple_of(tile * 8, 8)
 
         def plane(x, _):
-            base = (8 * tile + 2) * F
+            base = (8 * tile + H) * F
 
             def put(ref, at, modes):
                 for m in range(9):
@@ -373,11 +413,11 @@
                         ref[at, pl.ds(base + 8 + m, 8, stride=F), :] = im
 
             now = [stage[t, x, pl.ds(rows, 8), :] for t in range(16)]
-            put(sb, x + 2, real_dft([tws[t] * now[t] for t in range(16)]))
+            put(sb, x + H, real_dft([tws[t] * now[t] for t in range(16)]))
             before = [first[x, pl.ds(rows, 8), :]] + now[:15]
             put(
-                w,
-                x + 2,
+                w0,
+                x + H,
                 real_dft([tws[t] * (before[t] - now[t] * now[t] * now[t]) for t in range(16)]),
             )
             return 0
@@ -385,10 +425,10 @@
         lax.fori_loop(0, PL, plane, 0)
 
     def h_copy(d, tile):
-        rows = pl.ds(pl.multiple_of((8 * tile + 2) * F, 8), 8 * F)
-        return pltpu.make_async_remote_copy(
-            sb.at[2 if d == 0 else EP - 3, rows],
-            sb.at[EP - 2 if d == 0 else 1, rows],
+        rows = pl.ds(pl.multiple_of((8 * tile + H) * F, 8), 8 * F)
+        return pltpu.make_async_remote_copy(
+            sb.at[H if d == 0 else EP - 1 - H, rows],
+            sb.at[EP - H if d == 0 else H - 1, rows],
             h_s.at[d, tile],
             h_r.at[d, tile],
             device_id=(tm, gxs[d]),
@@ -397,154 +437,250 @@
 
     def hy_copy(d):
         return pltpu.make_async_remote_copy(
-            sb.at[pl.ds(2, PL), pl.ds((2 if d == 0 else ER - 3) * F, F)],
-            sb.at[pl.ds(2, PL), pl.ds((ER - 2 if d == 0 else 1) * F, F)],
+            sb.at[pl.ds(H, PL), pl.ds((H if d == 0 else ER - 1 - H) * F, F)],
+            sb.at[pl.ds(H, PL), pl.ds((ER - H if d == 0 else H - 1) * F, F)],
             hy_s.at[d],
             hy_r.at[d],
             device_id=(tms[d], gx),
             device_id_type=MESH,
         )
 
-    def x_copy(buf, par, d, e, i):
+    def hy_relay(d):
+        return pltpu.make_async_remote_copy(
+            sb.at[pl.ds(H, PL), pl.ds((H if d == 0 else ER - 1 - H) * F, F)],
+            passing_row,
+            hy_s.at[d],
+            p_r.at[STEPS],
+            device_id=(10 - tm, side),
+            device_id_type=MESH,
+        )
+
+    def hy_forward(d):
+        return pltpu.make_async_remote_copy(
+            passing_row,
+            sb.at[pl.ds(H, PL), pl.ds((ER - H if d == 0 else H - 1) * F, F)],
+            p_s.at[2],
+            hy_r.at[d],
+            device_id=(tm, side),
+            device_id_type=MESH,
+        )
+
+    def hy_start(d):
+        pl.when(y_to[d] & ~relayed[d])(lambda: hy_copy(d).start())
+        pl.when(relayed[d])(lambda: hy_relay(d).start())
+
+    def x_copy(ref, buf, par, d, e, i):
         r = R * i if e == 0 else ROWS - R - R * i
-        rows = pl.ds(pl.multiple_of((r + 2) * F, 8), R * F)
-        return pltpu.make_async_remote_copy(
-            w.at[pl.ds(buf + (2 if d == 0 else EP - 4), 2), rows],
-            w.at[pl.ds(buf + (EP - 2 if d == 0 else 0), 2), rows],
+        rows = pl.ds(pl.multiple_of((r + H) * F, 8), R * F)
+        return pltpu.make_async_remote_copy(
+            ref.at[pl.ds(buf + (H if d == 0 else PL), H), rows],
+            ref.at[pl.ds(buf + (EP - H if d == 0 else 0), H), rows],
             x_s.at[d, e, i],
             x_r.at[par, d, e, i],
             device_id=(tm, gxs[d]),
             device_id_type=MESH,
         )
 
-    def y_copy(buf, par, d):
-        return pltpu.make_async_remote_copy(
-            w.at[pl.ds(buf + 2, PL), pl.ds((2 if d == 0 else ER - 4) * F, 2 * F)],
-            w.at[pl.ds(buf + 2, PL), pl.ds((ER - 2 if d == 0 else 0) * F, 2 * F)],
+    def y_copy(ref, buf, par, d):
+        return pltpu.make_async_remote_copy(
+            ref.at[pl.ds(buf + H, PL), pl.ds((H if d == 0 else ROWS) * F, H * F)],
+            ref.at[pl.ds(buf + H, PL), pl.ds((ER - H if d == 0 else 0) * F, H * F)],
             y_s.at[d],
             y_r.at[par, d],
             device_id=(tms[d], gx),
             device_id_type=MESH,
         )
 
-    def c_copy(buf, par, d, e):
-        return pltpu.make_async_remote_copy(
-            w.at[buf + (2 if d == 0 else EP - 3), pl.ds((2 if e == 0 else ER - 3) * F, F)],
-            w.at[buf + (EP - 2 if d == 0 else 1), pl.ds((ER - 2 if e == 0 else 1) * F, F)],
+    def c_copy(ref, buf, par, d, e):
+        n = H - 1
+        return pltpu.make_async_remote_copy(
+            ref.at[pl.ds(buf + (H if d == 0 else PL + 1), n), pl.ds((H if e == 0 else ROWS + 1) * F, n * F)],
+            ref.at[pl.ds(buf + (EP - H if d == 0 else 1), n), pl.ds((ER - H if e == 0 else 1) * F, n * F)],
             c_s.at[d, e],
             c_r.at[par, d, e],
             device_id=(tms[e], gxs[d]),
             device_id_type=MESH,
         )
 
-    def x_start(buf, par, i):
+    def x_start(ref, buf, par, i):
         for e in range(2):
             for d in range(2):
-                pl.when(x_to[d])(lambda d=d, e=e: x_copy(buf, par, d, e, i).start())
-
-    def x_wait_send(buf, par, i):
+                pl.when(x_to[d])(lambda d=d, e=e: x_copy(ref, buf, par, d, e, i).start())
+
+    def x_wait_send(ref, buf, par, i):
         for e in range(2):
             for d in range(2):
-                pl.when(x_to[d])(lambda d=d, e=e: x_copy(buf, par, d, e, i).wait_send())
-
-    def x_wait_recv(buf, par, i):
+                pl.when(x_to[d])(lambda d=d, e=e: x_copy(ref, buf, par, d, e, i).wait_send())
+
+    def x_wait_recv(ref, buf, par, i):
         for e in range(2):
             for d in range(2):
-                pl.when(x_from[d])(lambda d=d, e=e: x_copy(buf, par, d, e, i).wait_recv())
-
-    def edges_start(buf, par):
+                pl.when(x_from[d])(lambda d=d, e=e: x_copy(ref, buf, par, d, e, i).wait_recv())
+
+    def y_relay(ref, buf, turn, d):
+        return pltpu.make_async_remote_copy(
+            ref.at[pl.ds(buf + H, PL), pl.ds((H if d == 0 else ROWS) * F, H * F)],
+            passing.at[turn],
+            y_s.at[d],
+            p_r.at[turn],
+            device_id=(10 - tm, side),
+            device_id_type=MESH,
+        )
+
+    def y_forward(ref, buf, turn, par, d):
+        return pltpu.make_async_remote_copy(
+            passing.at[turn],
+            ref.at[pl.ds(buf + H, PL), pl.ds((ER - H if d == 0 else 0) * F, H * F)],
+            p_s.at[0],
+            y_r.at[par, d],
+            device_id=(tm, side),
+            device_id_type=MESH,
+        )
+
+    def c_forward(ref, buf, turn, par, d, e):
+        n = H - 1
+        return pltpu.make_async_remote_copy(
+            passing.at[turn, pl.ds(0 if d == 0 else PL - n, n), pl.ds((0 if e == 0 else 1) * F, n * F)],
+            ref.at[pl.ds(buf + (EP - H if d == 0 else 1), n), pl.ds((ER - H if e == 0 else 1) * F, n * F)],
+            p_s.at[1],
+            c_r.at[par, d, e],
+            device_id=(tm, side_pair),
+            device_id_type=MESH,
+        )
+
+    def relay(ref, buf, turn, par, again):
+        for e in range(2):
+
+            @pl.when(relaying[e])
+            def _():
+                y_relay(ref, buf, turn, e).wait_recv()
+                if again:
+                    y_forward(ref, buf, turn, par, e).wait_send()
+                    c_forward(ref, buf, turn, par, 0, e).wait_send()
+                y_forward(ref, buf, turn, par, e).start()
+                pl.when(even)(lambda: c_forward(ref, buf, turn, par, 1, e).start())
+                pl.when(~even)(lambda: c_forward(ref, buf, turn, par, 0, e).start())
+
+    def edges_start(ref, buf, turn, par):
         for d in range(2):
-            pl.when(y_to[d])(lambda d=d: y_copy(buf, par, d).start())
+            pl.when(y_to[d] & ~relayed[d])(lambda d=d: y_copy(ref, buf, par, d).start())
+            pl.when(relayed[d])(lambda d=d: y_relay(ref, buf, turn, d).start())
         for d in range(2):
             for e in range(2):
-                pl.when(x_to[d] & y_to[e])(lambda d=d, e=e: c_copy(buf, par, d, e).start())
-
-    def edges_wait_send(buf, par):
+                pl.when(c_to[d][e])(lambda d=d, e=e: c_copy(ref, buf, par, d, e).start())
+
+    def edges_wait_send(ref, buf, par):
         for d in range(2):
-            pl.when(y_to[d])(lambda d=d: y_copy(buf, par, d).wait_send())
+            pl.when(y_to[d])(lambda d=d: y_copy(ref, buf, par, d).wait_send())
         for d in range(2):
             for e in range(2):
-                pl.when(x_to[d] & y_to[e])(lambda d=d, e=e: c_copy(buf, par, d, e).wait_send())
-
-    def edges_wait_recv(buf, par):
+                pl.when(c_to[d][e])(lambda d=d, e=e: c_copy(ref, buf, par, d, e).wait_send())
+
+    def edges_wait_recv(ref, buf, par):
         for d in range(2):
-            pl.when(y_from[d])(lambda d=d: y_copy(buf, par, d).wait_recv())
+            pl.when(y_from[d])(lambda d=d: y_copy(ref, buf, par, d).wait_recv())
         for d in range(2):
             for e in range(2):
                 pl.when(x_from[d] & y_from[e])(
-                    lambda d=d, e=e: c_copy(buf, par, d, e).wait_recv()
+                    lambda d=d, e=e: c_copy(ref, buf, par, d, e).wait_recv()
                 )
 
-    def row_parts(ref, base, yi, low, high):
+    def parts(ref, base, yi, low, high):
+        n = high - low
         at = pl.multiple_of(yi * 8, 8)
-        rows = [pl.multiple_of(yi * F + 8 * t, 8) for t in range(2)]
-
-        def get(px, t, dy):
-            return ref[base + px, pl.ds(pl.multiple_of(rows[t] + dy * F, 8), 8), :]
-
-        below = [get(low - 1, t, 0) for t in range(2)]
-        here = [get(low, t, 0) for t in range(2)]
-        face_low = fx[low, pl.ds(at, 8)]
-        for px in range(low, high):
-            face_high = fx[px + 1, pl.ds(at, 8)]
-            y_low = fy[px, pl.ds(at, 8)]
-            y_high = fy[px, pl.ds(pl.multiple_of(at + 8, 8), 8)]
-            z_low = fzl[px, pl.ds(at, 8)]
-            z_high = fzu[px, pl.ds(at, 8)]
+        near = ref.at[pl.ds(base + low - 1, n + 2), pl.ds(pl.multiple_of(yi * F - F, 8), 4 * F)]
+        vx = fx.at[pl.ds(low, n + 1), pl.ds(at, 16)]
+        vy = fy.at[pl.ds(low, n), pl.ds(at, 24)]
+        vl = fzl.at[pl.ds(low, n), pl.ds(at, 16)]
+        vu = fzu.at[pl.ds(low, n), pl.ds(at, 16)]
+
+        def get(i, r, t):
+            return near[i, pl.ds(r * F + 8 * t, 8), :]
+
+        def row(i):
+            return [[get(i, r, t) for t in range(2)] for r in (1, 2)]
+
+        below, here = row(0), row(1)
+        face_low = [vx[0, pl.ds(8 * r, 8), :] for r in range(2)]
+        for i in range(n):
+            above = row(i + 2)
+            face_high = [vx[i + 1, pl.ds(8 * r, 8), :] for r in range(2)]
+            face_y = [vy[i, pl.ds(8 * r, 8), :] for r in range(3)]
             sums = []
-            above = []
-            for t in range(2):
-                up = get(px + 1, t, 0)
-                above.append(up)
-                total = face_low * below[t] + face_high * up
-                total = total + (y_low * get(px, t, -1) + y_high * get(px, t, 1))
-                total = total + (
-                    z_low * pltpu.roll(here[t], 1, 1) + z_high * pltpu.roll(here[t], 127, 1)
-                )
-                sums.append(total)
-            yield px, at, rows, here, sums
+            for r in range(2):
+                z_low = vl[i, pl.ds(8 * r, 8), :]
+                z_high = vu[i, pl.ds(8 * r, 8), :]
+                pair = []
+                for t in range(2):
+                    y_low = get(i + 1, 0, t) if r == 0 else here[0][t]
+                    y_high = here[1][t] if r == 0 else get(i + 1, 3, t)
+                    pair.append(
+                        (face_low[r] * below[r][t] + face_high[r] * above[r][t])
+                        + (face_y[r] * y_low + face_y[r + 1] * y_high)
+                        + (
+                            z_low * pltpu.roll(here[r][t], 1, 1)
+                            + z_high * pltpu.roll(here[r][t], 127, 1)
+                        )
+                    )
+                sums.append(pair)
+            yield i, here, sums
             below, here, face_low = here, above, face_high
 
-    def divided(px, at, value):
-        a, b, c = ia[px, pl.ds(at, 8)], ib[px, pl.ds(at, 8)], ic[px, pl.ds(at, 8)]
-        return [a * value[0] - b * value[1], c * value[1] + b * value[0]]
+    def inverses(yi, low, high):
+        views = [
+            c.at[pl.ds(low, high - low), pl.ds(pl.multiple_of(yi * 8, 8), 16)] for c in (ia, ib, ic)
+        ]
+
+        def divided(i, r, value):
+            a, b, c = [v[i, pl.ds(8 * r, 8), :] for v in views]
+            return a * value[0] - b * value[1], c * value[1] + b * value[0]
+
+        return divided
 
     def starts(yi):
-        results = []
-        for px, at, rows, here, sums in row_parts(sb, 0, yi, 2, EP - 2):
-            diag = dg[px, pl.ds(at, 8)]
-            right = [
-                w[px, pl.ds(rows[t], 8), :] - (diag * here[t] - sums[t]) for t in range(2)
-            ]
-            results.append((px, rows, divided(px, at, right)))
-        for px, rows, value in results:
-            for t in range(2):
-                w[px, pl.ds(rows[t], 8), :] = value[t]
+        low, high = H, EP - H
+        divided = inverses(yi, low, high)
+        vd = dg.at[pl.ds(low, PL), pl.ds(pl.multiple_of(yi * 8, 8), 16)]
+        v0 = w0.at[pl.ds(low, PL), pl.ds(pl.multiple_of(yi * F, 8), 2 * F)]
+        for i, here, sums in parts(sb, 0, yi, low, high):
+            for r in range(2):
+                diag = vd[i, pl.ds(8 * r, 8), :]
+                spots = [pl.ds(r * F + 8 * t, 8) for t in range(2)]
+                right = [
+                    v0[i, spots[t], :] - (diag * here[r][t] - sums[r][t]) for t in range(2)
+                ]
+                value = divided(i, r, right)
+                for t in range(2):
+                    v0[i, spots[t], :] = value[t]
 
     def sweep(ref, base, target, target_base, yi, low, high, omega):
-        results = []
-        for px, at, rows, here, sums in row_parts(ref, base, yi, low, high):
-            step = divided(px, at, sums)
-            new = [
-                (1.0 - omega) * here[t] + omega * (w[px, pl.ds(rows[t], 8), :] + step[t])
-                for t in range(2)
-            ]
-            results.append((px, rows, new))
-        for px, rows, value in results:
-            for t in range(2):
-                target[target_base + px, pl.ds(rows[t], 8), :] = value[t]
+        divided = inverses(yi, low, high)
+        n = high - low
+        rows = pl.ds(pl.multiple_of(yi * F, 8), 2 * F)
+        v0 = w0.at[pl.ds(low, n), rows]
+        new = target.at[pl.ds(target_base + low, n), rows]
+        for i, here, sums in parts(ref, base, yi, low, high):
+            for r in range(2):
+                step = divided(i, r, sums[r])
+                for t in range(2):
+                    spot = pl.ds(r * F + 8 * t, 8)
+                    new[i, spot, :] = (1.0 - omega) * here[r][t] + omega * (
+                        v0[i, spot, :] + step[t]
+                    )
 
     def over(begin, count, body):
         def each(r, _):
-            body(begin + r + 2)
+            body(begin + 2 * r + H)
             return 0
 
-        lax.fori_loop(0, count, each, 0)
+        lax.fori_loop(0, count // 2, each, 0)
 
     def start_phase(i):
         over(R * i, R, starts)
         over(ROWS - R - R * i, R, starts)
-        x_start(0, 0, i)
+        if isinstance(i, int):
+            edges_start(w0, 0, 0, 0)
+        x_start(w0, 0, 0, i)
 
     for copy in own:
         copy.wait()
@@ -558,9 +694,16 @@
             for d in range(2):
                 pl.when(x_to[d])(lambda d=d, tile=tile: h_copy(d, tile).start())
             if tile == 0:
-                pl.when(y_to[0])(lambda: hy_copy(0).start())
+                hy_start(0)
             if tile == 3:
-                pl.when(y_to[1])(lambda: hy_copy(1).start())
+                hy_start(1)
+    for e in range(2):
+
+        @pl.when(relaying[e])
+        def _():
+            hy_relay(e).wait_recv()
+            hy_forward(e).start()
+
     for tiles in (TILE_ORDER[:2], TILE_ORDER[2:]):
         for tile in tiles:
             for d in range(2):
@@ -571,10 +714,10 @@
                 pl.when(y_from[0])(lambda: hy_copy(0).wait_recv())
         if tiles[0] == 0:
             start_phase(0)
-            edges_start(0, 0)
             lax.fori_loop(1, NPH // 2, lambda i, _: (start_phase(i), 0)[1], 0)
         else:
             lax.fori_loop(NPH // 2, NPH, lambda i, _: (start_phase(i), 0)[1], 0)
+    relay(w0, 0, 0, 0, False)
     for tile in range(4):
         for d in range(2):
             pl.when(x_to[d])(lambda d=d, tile=tile: h_copy(d, tile).wait_send())
@@ -612,8 +755,8 @@
         rows = pl.multiple_of(tile * 8, 8)
 
         def plane(x, _):
-            base = (8 * tile + 2) * F
-            field = [w[buf + x + 2, pl.ds(base + f, 8, stride=F), :] for f in range(F)]
+            base = (8 * tile + H) * F
+            field = [w[buf + x + H, pl.ds(base + f, 8, stride=F), :] for f in range(F)]
             modes = [(field[0], None)]
             modes += [(field[m], field[8 + m]) for m in range(1, 8)]
             modes += [(field[8], None)]
@@ -629,52 +772,67 @@
             home(tile, j).start()
         home_own(tile).start()
 
-    def two_sweeps(k, _):
+    def step(k, _):
         par = lax.rem(k, 2)
-        source = jnp.where(k == 0, 0, (1 + par) * EP)
-        result = (2 - par) * EP
-        om_a = pick(OMEGAS[0::2], k)
-        om_b = pick(OMEGAS[1::2], k)
-
-        def first_sweep(begin, count):
-            over(begin, count, lambda yi: sweep(w, source, wb, 0, yi, 1, EP - 1, om_a))
-
-        def second_sweep(begin, count):
-            over(begin, count, lambda yi: sweep(wb, 0, w, result, yi, 2, EP - 2, om_b))
+        source = par * EP
+        result = (1 - par) * EP
+        omegas = [pick(OMEGAS[turn::H], k) for turn in range(H)]
+
+        def sweeps(begins, counts):
+            for turn in range(H):
+                low, high = turn + 1, EP - turn - 1
+                for begin in begins[turn]:
+
+                    def run(ref, base, begin=begin, turn=turn, low=low, high=high):
+                        last = turn == H - 1
+                        target, target_base = (w, result) if last else (wb, turn * EP)
+                        over(
+                            begin,
+                            counts[turn],
+                            lambda yi: sweep(
+                                ref, base, target, target_base, yi, low, high, omegas[turn]
+                            ),
+                        )
+
+                    if turn == 0:
+                        pl.when(k == 0)(lambda: run(w0, 0))
+                        pl.when(k > 0)(lambda: run(w, source))
+                    else:
+                        run(wb, (turn - 1) * EP)
 
         def pass_on(i):
-            x_wait_send(result, par, i)
-
-            @pl.when(k < STEPS2 - 1)
+            x_wait_send(w, result, par, i)
+
+            @pl.when(k < STEPS - 1)
             def _():
-                x_start(result, 1 - par, i)
+                x_start(w, result, 1 - par, i)
 
         def finish(i):
-            @pl.when(k == STEPS2 - 1)
+            @pl.when(k == STEPS - 1)
             def _():
                 backward(result, i)
                 backward(result, 3 - i)
 
-        edges_wait_recv(source, par)
-        x_wait_recv(source, par, 0)
-        x_wait_recv(source, par, 1)
-        first_sweep(-1, R + 2)
-        first_sweep(ROWS - 1 - R, R + 2)
-        second_sweep(0, R)
-        second_sweep(ROWS - R, R)
+        rest = [H - 1 - turn for turn in range(H)]
+        edges_wait_recv(w, source, par)
+        x_wait_recv(w, source, par, 0)
+        x_wait_recv(w, source, par, 1)
+        sweeps([(-g, ROWS - R - g) for g in rest], [R + 2 * g for g in rest])
+        edges_wait_send(w, result, par)
+
+        @pl.when(k < STEPS - 1)
+        def _():
+            edges_start(w, result, k + 1, 1 - par)
+
         pass_on(0)
-        edges_wait_send(result, par)
-
-        @pl.when(k < STEPS2 - 1)
-        def _():
-            edges_start(result, 1 - par)
 
         def phase(i, _):
-            x_wait_recv(source, par, i + 1)
-            first_sweep(R * i + 1, R)
-            first_sweep(ROWS - 1 - R - R * i, R)
-            second_sweep(R * i, R)
-            second_sweep(ROWS - R - R * i, R)
+            x_wait_recv(w, source, par, i + 1)
+            sweeps([(R * i + g, ROWS - R - R * i - g) for g in rest], [R] * H)
+            @pl.when((i == NPH - 2) & (k < STEPS - 1))
+            def _():
+                relay(w, result, k + 1, 1 - par, True)
+
             pass_on(i)
 
             @pl.when(i == NPH // 2 - 1)
@@ -684,13 +842,20 @@
             return 0
 
         lax.fori_loop(1, NPH - 1, phase, 0)
-        first_sweep(17 - R, 2 * R - 2)
-        second_sweep(16 - R, 2 * R)
+        sweeps([(16 - R + g,) for g in rest], [2 * R - 2 * g for g in rest])
         pass_on(NPH - 1)
         finish(1)
         return 0
 
-    lax.fori_loop(0, STEPS2, two_sweeps, 0)
+    lax.fori_loop(0, STEPS, step, 0)
+
+    for e in range(2):
+
+        @pl.when(relaying[e])
+        def _():
+            hy_forward(e).wait_send()
+            y_forward(w, 0, 0, 0, e).wait_send()
+            c_forward(w, 0, 0, 0, 0, e).wait_send()
 
     for j in range(7):
         weight_out(j).wait_send()
@@ -705,17 +870,20 @@
 
 def shards(ngx, state, start_field, diffusivity, time_weights, shift_real, shift_imag):
     dma = pltpu.SemaphoreType.DMA
-    any_space = pl.BlockSpec(memory_space=pl.ANY)
-    smem = pl.BlockSpec(memory_space=pltpu.SMEM)
+    hbm = pl.BlockSpec(memory_space=pltpu.HBM)
     coefficient = pltpu.VMEM((EP, ER * 8, 128), F32)
     return pl.pallas_call(
         functools.partial(kernel, ngx),
         out_shape=jax.ShapeDtypeStruct(state.shape, F32),
-        in_specs=[any_space, any_space, any_space, smem, smem, smem],
-        out_specs=any_space,
+        in_specs=[hbm] * 6,
+        out_specs=hbm,
         scratch_shapes=[
-            pltpu.VMEM((3 * EP, ER * F, 128), F32),
+            pltpu.SMEM((2,), F32),
+            pltpu.SMEM((16,), F32),
+            pltpu.SMEM((16,), F32),
+            pltpu.VMEM((2 * EP, ER * F, 128), F32),
             pltpu.VMEM((EP, ER * F, 128), F32),
+            pltpu.VMEM(((H - 1) * EP, ER * F, 128), F32),
             pltpu.VMEM((EP, ER * F, 128), F32),
             pltpu.VMEM((16, PL, ROWS, 128), F32),
             pltpu.VMEM((PL, ROWS, 128), F32),
@@ -725,7 +893,7 @@
         ]
         + [coefficient] * 8
         + [
-            dma((5,)),
+            dma((8,)),
             dma((7, 4)),
             dma((7, 4)),
             dma((7,)),
@@ -745,9 +913,13 @@
             dma((7, 4)),
             dma((7, 4)),
             dma((4,)),
+            pltpu.VMEM((STEPS, PL, H * F, 128), F32),
+            pltpu.VMEM((PL, F, 128), F32),
+            dma((3,)),
+            dma((STEPS + 1,)),
         ],
         compiler_params=pltpu.CompilerParams(
-            collective_id=0, has_side_effects=True, vmem_limit_bytes=44 * 2**20
+            collective_id=0, has_side_effects=True, vmem_limit_bytes=56 * 2**20
         ),
         cost_estimate=pl.CostEstimate(
             flops=200_000_000, bytes_accessed=4 * 2**20, transcendentals=0

time: 113 us -> 96.1 us (0.85); the launches traced: 113 us -> 94.4 us
  Pallas kernels: 107 us -> 92.1 us
  local copies, waits for them, and re-layouts: 6.24 us -> 2.27 us
    pallas_call x1, Pallas kernels: 107 us -> 92.1 us  [shards(): pl.pallas_call(functools.partial(kernel, ngx), out_shape=jax.ShapeDtypeSt...]
    unnamed x13 -> x1, local copies, waits for them, and re-layouts: 6.24 us -> 2.27 us
where the time goes in v2:
time: 96.1 us; the launch traced here: 94.4 us
  Pallas kernels  92.1 us (96%)
  local copies, waits for them, and re-layouts  2.27 us (2%)
    pallas_call x1, Pallas kernels, shards(): pl.pallas_call(functools.partial(kernel, ngx), out_shape=jax.ShapeDtypeSt...  92.1 us
    unnamed x1, local copies, waits for them, and re-layouts  2.27 us

profile of v2, /device:TPU:1, one launch (start us, length us, event | category | flops | bytes accessed | tf_op | source)
XLA Modules:
  0.0 94.4 jit_solution(4925726893429192117)
XLA Ops:
  0.0 92.1 %shard_map.64 = f32[2,4,256,128]{3,2,1,0:T(8,128)} custom-call(f32[2,4,256,128]{3,2,1,0:T(8,128)} %state.1, f32[4,256,128]{2,1,0:T(8,128)} %start.1, f32[4,256,128]{2,1,0:T(8,128)} %kappa.1, f32[2]{0:T(128)} %weights_in.1, f32[16]{0:T(128)} %shift_real_in.1, f32[16]{0:T(128)} %shift_imag_in.1), custom_call_target="tpu_custom_call" | custom-call | flops 200000000 | bytes 4194304 | tf_op jit(solution)/shard_map/pallas_call | solution.py:875
  92.1 2.3 %copy.8 = f32[2,4,256,128]{3,2,1,0:T(8,128)} copy(f32[2,4,256,128]{3,2,1,0:T(8,128)} %shard_map.64) | data formatting | bytes 2097152

commit v3 on v2

--- a/solution.py
+++ b/solution.py
@@ -18,7 +18,7 @@
 TMS = 8
 PL = 4
 ROWS = 32
-H = 3
+H = 4
 EP = PL + 2 * H
 ER = ROWS + 2 * H
 F = 16

time: 96.1 us -> 99.3 us (1.033)
  Pallas kernels: 92.1 us -> 96 us
    pallas_call x1, Pallas kernels: 92.1 us -> 96 us  [shards(): pl.pallas_call(functools.partial(kernel, ngx), out_shape=jax.ShapeDtypeSt...]
where the time goes in v3:
time: 99.3 us; the launch traced here: 98.3 us
  Pallas kernels  96 us (97%)
  local copies, waits for them, and re-layouts  2.27 us (2%)
    pallas_call x1, Pallas kernels, shards(): pl.pallas_call(functools.partial(kernel, ngx), out_shape=jax.ShapeDtypeSt...  96 us
    unnamed x1, local copies, waits for them, and re-layouts  2.27 us

profile of v3, /device:TPU:1, one launch (start us, length us, event | category | flops | bytes accessed | tf_op | source)
XLA Modules:
  0.0 98.3 jit_solution(3550964157288312044)
XLA Ops:
  0.0 96.0 %shard_map.64 = f32[2,4,256,128]{3,2,1,0:T(8,128)} custom-call(f32[2,4,256,128]{3,2,1,0:T(8,128)} %state.1, f32[4,256,128]{2,1,0:T(8,128)} %start.1, f32[4,256,128]{2,1,0:T(8,128)} %kappa.1, f32[2]{0:T(128)} %weights_in.1, f32[16]{0:T(128)} %shift_real_in.1, f32[16]{0:T(128)} %shift_imag_in.1), custom_call_target="tpu_custom_call" | custom-call | flops 200000000 | bytes 4194304 | tf_op jit(solution)/shard_map/pallas_call | solution.py:875
  96.0 2.3 %copy.8 = f32[2,4,256,128]{3,2,1,0:T(8,128)} copy(f32[2,4,256,128]{3,2,1,0:T(8,128)} %shard_map.64) | data formatting | bytes 2097152
